TPU v7x, 128 devices: a whole 4x4x4 slice. The times are simulated.
128 devices in a mesh: sub: 32 (over z, x, core), grp: 4 (over y).
Axes of the slice: x: 4, y: 4, z: 4, core: 2. Of those that a mesh axis runs over, the one named last changes fastest.
Arguments:
- residual: float32 [32, 128, 4608], P('sub', None, 'grp'), may hold values from -8 to 8
- neumann: bfloat16 [32, 4608, 4608], P('sub', 'grp'), may hold values from -0.09375 to 0.09375
- projection: bfloat16 [32, 4, 4, 768, 1024], P('sub', 'grp'), may hold values from -0.21875 to 0.21875
- pair_list: int32 [32, 4, 4, 2], replicated, may hold values from 0 to 31, as said below
- slave_dofs: int32 [32, 4, 2, 768], P('sub', 'grp'), may hold values from 0 to 1151, as said below
- master_dofs: int32 [32, 4, 4, 1024], P('sub', 'grp'), may hold values from 0 to 1151, as said below
- zbasis: float32 [32, 48, 4608], P('sub'), may hold values from -0.09375 to 0.09375
- ybasis: float32 [32, 48, 4608], P('sub'), may hold values from -0.21875 to 0.21875
- coarse_inverse: float32 [768, 768], replicated, may hold values from -0.21875 to 0.21875
- coarse_ids: int32 [32], P('sub'), may hold values from 0 to 15
Outputs:
- balanced: float32 [32, 128, 4608], P('sub', None, 'grp')
- correction: float32 [32, 128, 4608], P('sub', None, 'grp')
Inputs may be any that keep to these rules, and one draw needn't show every extreme that they name: `pair_list`: entry [s, g, j] holds the slave subdomain b of pair j of region g of subdomain s, then the number of b's slave face in region g. b is s + k modulo 32 for some k with 1 <= |k| <= 2; in each region no k is used by more than 2 pairs, and at least one k is used by exactly 2. `slave_dofs`: each face lists distinct positions within its region. `master_dofs`: each face lists distinct positions within its region.
All inputs are finite; a program needn't handle non-finite values.
Results may differ from a plain program's by a relative error of at most 0.0041.
Values may be sent and summed in bfloat16 or wider, within the bound.
A program may use at most 128 MiB of HBM per device.

v0:
```python
import jax
import jax.numpy as jnp
from jax import lax
from jax.sharding import PartitionSpec as P

FS = 768
NC = 48
PAIRS = 4
SFACES = 2
RANGE = 2
CAP = 2
CBLK = 16


def passed_along(value, axis, steps):
    count = lax.axis_size(axis)
    pairs = [(source, (source + steps) % count) for source in range(count)]
    return lax.ppermute(value, axis, pairs)


def signed_gap(slave_sub, owner_sub, sub_count):
    return (slave_sub - owner_sub + sub_count // 2) % sub_count - sub_count // 2


def rank_within(gap_list):
    same = gap_list[:, None] == gap_list[None, :]
    earlier = jnp.arange(PAIRS)[:, None] < jnp.arange(PAIRS)[None, :]
    return jnp.sum(jnp.where(same & earlier, 1, 0), axis=0).astype(jnp.int32)


def list_of(pair_list, owner_sub, group_at):
    return lax.dynamic_slice(pair_list, (owner_sub, group_at, 0, 0), (1, 1, PAIRS, 2))[0, 0]


def contract_last(left_side, right_side):
    return lax.dot_general(
        left_side, right_side, (((1,), (1,)), ((), ())), preferred_element_type=jnp.float32
    )


def exact_last(left_side, right_side):
    return lax.dot_general(
        left_side, right_side, (((1,), (1,)), ((), ())), precision=lax.Precision.HIGHEST
    )


def exact_first(left_side, right_side):
    return lax.dot_general(
        left_side, right_side, (((0,), (0,)), ((), ())), precision=lax.Precision.HIGHEST
    )


def local(
    residual,
    neumann,
    projection,
    pair_list,
    slave_dofs,
    master_dofs,
    zbasis,
    ybasis,
    coarse_inverse,
    coarse_ids,
):
    highest = lax.Precision.HIGHEST
    sub_count = lax.axis_size("sub")
    my_sub = lax.axis_index("sub")
    group_at = lax.axis_index("grp")
    region = residual[0]
    columns, row_count = region.shape
    reach = [step - RANGE for step in range(RANGE)] + [step + 1 for step in range(RANGE)]
    my_faces = slave_dofs[0, 0]
    outgoing = []
    targets = []
    for offset in reach:
        owner_sub = (my_sub - offset) % sub_count
        owner_list = list_of(pair_list, owner_sub, group_at)
        gap_list = signed_gap(owner_list[:, 0], owner_sub, sub_count)
        order_in = rank_within(gap_list)
        traces = []
        for slot_at in range(CAP):
            matched = (gap_list == offset) & (order_in == slot_at)
            face_id = jnp.sum(jnp.where(matched, owner_list[:, 1], 0))
            dof_idx = jnp.sum(
                jnp.where(jnp.arange(SFACES)[:, None] == face_id, my_faces, 0), axis=0
            )
            is_live = jnp.any(matched)
            traces.append(
                jnp.where(is_live, jnp.take(region, dof_idx, axis=1), 0.0).astype(jnp.bfloat16)
            )
            targets.append((dof_idx, is_live))
        outgoing.append(jnp.stack(traces))
    arrived = [passed_along(outgoing[spot], "sub", -offset) for spot, offset in enumerate(reach)]
    stacked = jnp.stack(arrived)
    own_list = list_of(pair_list, my_sub, group_at)
    own_gaps = signed_gap(own_list[:, 0], my_sub, sub_count)
    own_ranks = rank_within(own_gaps)
    positions = jnp.where(own_gaps < 0, own_gaps + RANGE, own_gaps + RANGE - 1)
    updated = region
    replies = jnp.zeros((2 * RANGE, CAP, columns, FS), jnp.bfloat16)
    for column in range(PAIRS):
        slave_trace = lax.dynamic_slice(
            stacked, (positions[column], own_ranks[column], 0, 0), (1, 1, columns, FS)
        )[0, 0]
        matrix = projection[0, 0, column]
        master_idx = master_dofs[0, 0, column]
        mismatch = jnp.dot(slave_trace, matrix, preferred_element_type=jnp.float32) - jnp.take(
            region, master_idx, axis=1
        )
        updated = updated.at[:, master_idx].add(0.5 * mismatch)
        returned = contract_last(mismatch.astype(jnp.bfloat16), matrix).astype(jnp.bfloat16)
        placed = (jnp.arange(2 * RANGE)[:, None] == positions[column]) & (
            jnp.arange(CAP)[None, :] == own_ranks[column]
        )
        replies = replies + jnp.where(
            placed[:, :, None, None], returned, jnp.zeros((), jnp.bfloat16)
        )
    answers = [passed_along(replies[spot], "sub", offset) for spot, offset in enumerate(reach)]
    for spot in range(len(reach)):
        for slot_at in range(CAP):
            dof_idx, is_live = targets[spot * CAP + slot_at]
            updated = updated.at[:, dof_idx].add(
                jnp.where(is_live, -0.5 * answers[spot][slot_at].astype(jnp.float32), 0.0)
            )
    selector = (jnp.arange(CBLK) == coarse_ids[0]).astype(jnp.float32)
    zfull = zbasis[0]
    yfull = ybasis[0]
    inverse_rows = neumann[0]
    zpart = lax.dynamic_slice_in_dim(zfull, group_at * row_count, row_count, 1)
    local_part = exact_last(zpart, updated)
    coarse_sum = lax.psum(selector[:, None, None] * local_part[None], ("sub", "grp"))
    flat = coarse_sum.reshape(CBLK * NC, columns)
    multipliers = jnp.dot(coarse_inverse, flat, precision=highest).reshape(CBLK, NC, columns)
    chosen_mult = jnp.sum(selector[:, None, None] * multipliers, axis=0)
    ypart = lax.dynamic_slice_in_dim(yfull, group_at * row_count, row_count, 1)
    neumann_input = (updated - exact_first(chosen_mult, ypart)).astype(jnp.bfloat16)
    solved = contract_last(lax.all_gather(neumann_input, "grp", axis=1, tiled=True), inverse_rows)
    correction = exact_first(chosen_mult, zpart) + solved
    return (updated[None], correction[None])


def solution(mesh):
    placed = (
        P("sub", None, "grp"),
        P("sub", "grp", None),
        P("sub", "grp", None, None, None),
        P(),
        P("sub", "grp", None, None),
        P("sub", "grp", None, None),
        P("sub", None, None),
        P("sub", None, None),
        P(),
        P("sub"),
    )
    return jax.shard_map(
        local,
        mesh=mesh,
        in_specs=placed,
        out_specs=(P("sub", None, "grp"), P("sub", None, "grp")),
        check_vma=False,
    )
```

profile of v0, /device:TPU:0, one launch (start us, length us, event | category | flops | bytes accessed | tf_op | source)
XLA Modules:
  0.0 432.2 jit_solution(14092798572127664321)
XLA Ops:
  39.8 5.1 %collective-permute-start.2 = (bf16[2,128,768]{1,2,0:T(8,128)(2,1)}, bf16[2,128,768]{1,2,0:T(8,128)(2,1)}, u32[]{:S(2)}, u32[]{:S(2)}) collective-permute-start(bf16[2,128,768]{1,2,0:T(8,128)(2,1)} %pad_maximum_fusion.3), channel_id=1, source_target_pairs={{0,124},{4,0},{8,4},{12,8},{16,12},{20,16},{24,20},{28,24},{32,28}... | collective-permute-start | bytes 1179656 | tf_op jit(solution)/shard_map/ppermute | solution.py:18
  75.4 2.8 gather_fusion.11
  79.2 4.0 gather_fusion.10
  84.4 4.0 gather_fusion.9
  90.5 4.0 gather_fusion.8
  113.8 2.8 fusion.46
  125.1 2.7 fusion.43
  140.3 5.1 %collective-permute-start.5 = (bf16[2,128,768]{1,2,0:T(8,128)(2,1)}, bf16[2,128,768]{1,2,0:T(8,128)(2,1)}, u32[]{:S(2)}, u32[]{:S(2)}) collective-permute-start(bf16[2,128,768]{1,2,0:T(8,128)(2,1)} %get-tuple-element.38), channel_id=1, source_target_pairs={{0,124},{4,0},{8,4},{12,8},{16,12},{20,16},{24,20},{28,24},{32,28}... | collective-permute-start | bytes 1179656 | tf_op jit(solution)/shard_map/ppermute | solution.py:18
  152.8 6.7 %scatter_fusion = f32[128,1152]{0,1:T(8,128)S(1)} fusion(f32[128,1152]{0,1:T(8,128)S(1)} %bitcast.338, s32[1024]{0:T(1024)S(1)} %bitcast.353, f32[1024,128]{1,0:T(8,128)} %copy.59), kind=kCustom, calls=%fused_computation.12 | custom fusion | flops 131072 | bytes 1576960 | tf_op jit(solution)/shard_map/scatter-add | solution.py:110
  159.4 6.3 %scatter_fusion.1 = f32[128,1152]{0,1:T(8,128)S(1)} fusion(f32[128,1152]{0,1:T(8,128)S(1)} %scatter_fusion, s32[1024]{0:T(1024)S(1)} %bitcast.352, f32[1024,128]{1,0:T(8,128)S(1)} %copy.61), kind=kCustom, calls=%fused_computation.13 | custom fusion | flops 131072 | bytes 1576960 | tf_op jit(solution)/shard_map/scatter-add | solution.py:110
  165.7 6.9 %scatter_fusion.2 = f32[128,1152]{0,1:T(8,128)S(1)} fusion(f32[128,1152]{0,1:T(8,128)S(1)} %scatter_fusion.1, s32[1024]{0:T(1024)S(1)} %bitcast.351, f32[1024,128]{1,0:T(8,128)} %copy.63), kind=kCustom, calls=%fused_computation.14 | custom fusion | flops 131072 | bytes 1576960 | tf_op jit(solution)/shard_map/scatter-add | solution.py:110
  172.6 6.3 %scatter_fusion.3 = f32[128,1152]{0,1:T(8,128)S(1)} fusion(f32[128,1152]{0,1:T(8,128)S(1)} %scatter_fusion.2, s32[1024]{0:T(1024)S(1)} %bitcast.350, f32[1024,128]{1,0:T(8,128)S(1)} %copy-done.4), kind=kCustom, calls=%fused_computation.15 | custom fusion | flops 131072 | bytes 1576960 | tf_op jit(solution)/shard_map/scatter-add | solution.py:110
  178.9 7.3 %scatter_custom_fusion.4 = f32[128,1152]{0,1:T(8,128)S(1)} fusion(f32[128,1152]{0,1:T(8,128)S(1)} %scatter_fusion.3, s32[768]{0:T(1024)S(1)} %fusion.171, bf16[2,128,768]{1,2,0:T(8,128)(2,1)} %collective-permute-done.4, f32[]{:T(128)} %constant.147.clone.1, f32[]{:T(128)} %constant.153.clone.1, pred[]{:T(512)} %get-tuple-element.26), kind=kCustom, calls=%fused_computation.91 | custom fusion | flops 393216 | bytes 787968 | tf_op jit(solution)/shard_map/scatter-add | solution.py:122
  186.2 7.3 %scatter_custom_fusion.5 = f32[128,1152]{0,1:T(8,128)S(1)} fusion(f32[128,1152]{0,1:T(8,128)S(1)} %scatter_custom_fusion.4, s32[768]{0:T(1024)S(1)} %get-tuple-element.85, bf16[2,128,768]{1,2,0:T(8,128)(2,1)} %collective-permute-done.4, f32[]{:T(128)} %constant.147.clone.1, f32[]{:T(128)} %constant.153.clone.1, pred[]{:T(512)} %get-tuple-element.27), kind=kCustom, calls=%fused_computation.89 | custom fusion | flops 393216 | bytes 787968 | tf_op jit(solution)/shard_map/scatter-add | solution.py:122
  193.5 7.4 %scatter_custom_fusion.6 = f32[128,1152]{0,1:T(8,128)S(1)} fusion(f32[128,1152]{0,1:T(8,128)S(1)} %scatter_custom_fusion.5, s32[768]{0:T(1024)S(1)} %get-tuple-element.86, bf16[2,128,768]{1,2,0:T(8,128)(2,1)} %collective-permute-done.5, f32[]{:T(128)} %constant.147.clone.1, f32[]{:T(128)} %constant.153.clone.1, pred[]{:T(512)} %get-tuple-element.28), kind=kCustom, calls=%fused_computation.87 | custom fusion | flops 393216 | bytes 787968 | tf_op jit(solution)/shard_map/scatter-add | solution.py:122
  200.9 7.6 %scatter_custom_fusion.7 = f32[128,1152]{0,1:T(8,128)S(1)} fusion(f32[128,1152]{0,1:T(8,128)S(1)} %scatter_custom_fusion.6, s32[768]{0:T(1024)S(1)} %fusion.174, bf16[2,128,768]{1,2,0:T(8,128)(2,1)} %collective-permute-done.5, f32[]{:T(128)} %constant.147.clone.1, f32[]{:T(128)} %constant.153.clone.1, pred[]{:T(512)} %get-tuple-element.29), kind=kCustom, calls=%fused_computation.85 | custom fusion | flops 393216 | bytes 787968 | tf_op jit(solution)/shard_map/scatter-add | solution.py:122
  208.6 7.3 %scatter_custom_fusion.8 = f32[128,1152]{0,1:T(8,128)S(1)} fusion(f32[128,1152]{0,1:T(8,128)S(1)} %scatter_custom_fusion.7, s32[768]{0:T(1024)S(1)} %fusion.175, bf16[2,128,768]{1,2,0:T(8,128)(2,1)} %collective-permute-done.6, f32[]{:T(128)} %constant.147.clone.1, f32[]{:T(128)} %constant.153.clone.1, pred[]{:T(512)} %get-tuple-element.30), kind=kCustom, calls=%fused_computation.83 | custom fusion | flops 393216 | bytes 787968 | tf_op jit(solution)/shard_map/scatter-add | solution.py:122
  215.8 7.4 %scatter_custom_fusion.9 = f32[128,1152]{0,1:T(8,128)S(1)} fusion(f32[128,1152]{0,1:T(8,128)S(1)} %scatter_custom_fusion.8, s32[768]{0:T(1024)S(1)} %fusion.176, bf16[2,128,768]{1,2,0:T(8,128)(2,1)} %collective-permute-done.6, f32[]{:T(128)} %constant.147.clone.1, f32[]{:T(128)} %constant.153.clone.1, pred[]{:T(512)} %get-tuple-element.31), kind=kCustom, calls=%fused_computation.81 | custom fusion | flops 393216 | bytes 787968 | tf_op jit(solution)/shard_map/scatter-add | solution.py:122
  223.2 7.2 %scatter_custom_fusion.10 = f32[128,1152]{0,1:T(8,128)S(1)} fusion(f32[128,1152]{0,1:T(8,128)S(1)} %scatter_custom_fusion.9, s32[768]{0:T(1024)S(1)} %get-tuple-element.87, bf16[2,128,768]{1,2,0:T(8,128)(2,1)} %collective-permute-done.7, f32[]{:T(128)} %constant.147.clone.1, f32[]{:T(128)} %constant.153.clone.1, pred[]{:T(512)} %get-tuple-element.32), kind=kCustom, calls=%fused_computation.79 | custom fusion | flops 393216 | bytes 787968 | tf_op jit(solution)/shard_map/scatter-add | solution.py:122
  230.5 7.5 %scatter_custom_fusion.11 = f32[128,1152]{0,1:T(8,128)S(1)} fusion(f32[128,1152]{0,1:T(8,128)S(1)} %scatter_custom_fusion.10, s32[768]{0:T(1024)S(1)} %get-tuple-element.88, bf16[2,128,768]{1,2,0:T(8,128)(2,1)} %collective-permute-done.7, f32[]{:T(128)} %constant.147.clone.1, f32[]{:T(128)} %constant.153.clone.1, pred[]{:T(512)} %get-tuple-element.33), kind=kCustom, calls=%fused_computation.77 | custom fusion | flops 393216 | bytes 787968 | tf_op jit(solution)/shard_map/scatter-add | solution.py:122
  240.6 141.8 %all-reduce.2.cloned.1.call-done = f32[768,128]{1,0:T(8,128)} async-done(((f32[768,128]{1,0:T(8,128)}), f32[768,128]{1,0:T(8,128)}) %all-reduce.2.cloned.1.call-update) | async-done | bytes 393232 | tf_op jit(solution)/shard_map/psum | solution.py:131
  382.4 3.8 convolution_bitcast_fusion
  393.2 21.7 %all-gather.2.cloned.1.call-done = bf16[128,4608]{1,0:T(8,128)(2,1)} async-done(((bf16[128,1152]{1,0:T(8,128)(2,1)}), bf16[128,4608]{1,0:T(8,128)(2,1)}) %all-gather.2.cloned.1.call-update) | async-done | bytes 1179664 | tf_op jit(solution)/shard_map/all_gather | solution.py:137
  414.9 7.8 %fusion = f32[128,1152]{1,0:T(8,128)S(1)} fusion(bf16[128,4608]{1,0:T(8,128)(2,1)} %all-gather.2.cloned.1.call-done, bf16[1,1152,4608]{2,1,0:T(8,128)(2,1)} %param.15), kind=kOutput, calls=%fused_computation.24 | convolution fusion | flops 1358954496 | bytes 12386304 | tf_op jit(solution)/shard_map/dot_general | solution.py:36
  (188 shorter events, 110.4 us)
Async XLA Ops:
  7.2 375.2 %copy-start = (f32[768,768]{1,0:T(8,128)S(1)}, f32[768,768]{1,0:T(8,128)}, u32[]{:S(2)}) copy-start(f32[768,768]{1,0:T(8,128)} %param.22) | copy-start | bytes 7077892
  7.2 375.2 %all-reduce.2.cloned.1.call-start = ((), (), s32[]{:S(2)}) async-start(), calls=%async_computation | async-start | bytes 786432 | tf_op jit(solution)/shard_map/psum | solution.py:131
  25.5 78.9 %collective-permute-start = (bf16[2,128,768]{1,2,0:T(8,128)(2,1)}, bf16[2,128,768]{1,2,0:T(8,128)(2,1)}, u32[]{:S(2)}, u32[]{:S(2)}) collective-permute-start(bf16[2,128,768]{1,2,0:T(8,128)(2,1)} %pad_maximum_fusion.1), channel_id=1, source_target_pairs={{0,8},{4,12},{8,16},{12,20},{16,24},{20,28},{24,32},{28,36},{32,40... | collective-permute-start | bytes 1179656 | tf_op jit(solution)/shard_map/ppermute | solution.py:18
  33.4 71.0 %collective-permute-start.1 = (bf16[2,128,768]{1,2,0:T(8,128)(2,1)}, bf16[2,128,768]{1,2,0:T(8,128)(2,1)}, u32[]{:S(2)}, u32[]{:S(2)}) collective-permute-start(bf16[2,128,768]{1,2,0:T(8,128)(2,1)} %pad_maximum_fusion.2), channel_id=1, source_target_pairs={{0,4},{4,8},{8,12},{12,16},{16,20},{20,24},{24,28},{28,32},{32,36}... | collective-permute-start | bytes 1179656 | tf_op jit(solution)/shard_map/ppermute | solution.py:18
  39.8 64.6 %collective-permute-start.2 = (bf16[2,128,768]{1,2,0:T(8,128)(2,1)}, bf16[2,128,768]{1,2,0:T(8,128)(2,1)}, u32[]{:S(2)}, u32[]{:S(2)}) collective-permute-start(bf16[2,128,768]{1,2,0:T(8,128)(2,1)} %pad_maximum_fusion.3), channel_id=1, source_target_pairs={{0,124},{4,0},{8,4},{12,8},{16,12},{20,16},{24,20},{28,24},{32,28}... | collective-permute-start | bytes 1179656 | tf_op jit(solution)/shard_map/ppermute | solution.py:18
  47.2 5.6 %copy-start.9 = (s32[1,1,4,1024]{3,2,1,0:T(4,128)S(1)}, s32[1,1,4,1024]{3,2,1,0:T(4,128)}, u32[]{:S(2)}) copy-start(s32[1,1,4,1024]{3,2,1,0:T(4,128)} %param.19) | copy-start | bytes 49156
  51.2 53.2 %collective-permute-start.3 = (bf16[2,128,768]{1,2,0:T(8,128)(2,1)}, bf16[2,128,768]{1,2,0:T(8,128)(2,1)}, u32[]{:S(2)}, u32[]{:S(2)}) collective-permute-start(bf16[2,128,768]{1,2,0:T(8,128)(2,1)} %pad_maximum_fusion.4), channel_id=1, source_target_pairs={{0,120},{4,124},{8,0},{12,4},{16,8},{20,12},{24,16},{28,20},{32,24... | collective-permute-start | bytes 1179656 | tf_op jit(solution)/shard_map/ppermute | solution.py:18
  90.5 11.2 %copy-start.17 = (pred[4]{0:T(512)(128)(4,1)S(1)}, pred[4]{0:T(512)(128)(4,1)}, u32[]{:S(2)}) copy-start(pred[4]{0:T(512)(128)(4,1)} %iota_compare_fusion.2) | copy-start | bytes 16
  90.5 12.4 %copy-start.15 = (pred[4]{0:T(512)(128)(4,1)S(1)}, pred[4]{0:T(512)(128)(4,1)}, u32[]{:S(2)}) copy-start(pred[4]{0:T(512)(128)(4,1)} %iota_compare_fusion.6) | copy-start | bytes 16
  90.5 12.4 %copy-start.16 = (pred[4]{0:T(512)(128)(4,1)S(1)}, pred[4]{0:T(512)(128)(4,1)}, u32[]{:S(2)}) copy-start(pred[4]{0:T(512)(128)(4,1)} %iota_compare_fusion.8) | copy-start | bytes 16
  106.0 6.0 %copy-start.2 = (bf16[4,2,128,768]{2,3,1,0:T(8,128)(2,1)}, bf16[4,2,128,768]{2,3,1,0:T(8,128)(2,1)S(1)}, u32[]{:S(2)}) copy-start(bf16[4,2,128,768]{2,3,1,0:T(8,128)(2,1)S(1)} %pad_maximum_fusion) | copy-start | bytes 4718596
  118.4 3.8 copy-start.6
  132.3 4.5 %copy-start.11 = (pred[4,2]{1,0:T(4,128)(4,1)S(1)}, pred[4,2]{1,0:T(4,128)(4,1)}, u32[]{:S(2)}) copy-start(pred[4,2]{1,0:T(4,128)(4,1)} %get-tuple-element.89) | copy-start | bytes 28
  132.3 4.5 %copy-start.12 = (pred[4,2]{1,0:T(4,128)(4,1)S(1)}, pred[4,2]{1,0:T(4,128)(4,1)}, u32[]{:S(2)}) copy-start(pred[4,2]{1,0:T(4,128)(4,1)} %get-tuple-element.90) | copy-start | bytes 28
  132.3 4.5 %copy-start.13 = (pred[4,2]{1,0:T(4,128)(4,1)S(1)}, pred[4,2]{1,0:T(4,128)(4,1)}, u32[]{:S(2)}) copy-start(pred[4,2]{1,0:T(4,128)(4,1)} %get-tuple-element.91) | copy-start | bytes 28
  132.4 4.5 %copy-start.14 = (pred[4,2]{1,0:T(4,128)(4,1)S(1)}, pred[4,2]{1,0:T(4,128)(4,1)}, u32[]{:S(2)}) copy-start(pred[4,2]{1,0:T(4,128)(4,1)} %get-tuple-element.92) | copy-start | bytes 28
  139.7 83.5 %collective-permute-start.7 = (bf16[2,128,768]{1,2,0:T(8,128)(2,1)}, bf16[2,128,768]{1,2,0:T(8,128)(2,1)}, u32[]{:S(2)}, u32[]{:S(2)}) collective-permute-start(bf16[2,128,768]{1,2,0:T(8,128)(2,1)} %get-tuple-element.36), channel_id=1, source_target_pairs={{0,8},{4,12},{8,16},{12,20},{16,24},{20,28},{24,32},{28,36},{32,40... | collective-permute-start | bytes 1179656 | tf_op jit(solution)/shard_map/ppermute | solution.py:18
  140.3 68.2 %collective-permute-start.6 = (bf16[2,128,768]{1,2,0:T(8,128)(2,1)}, bf16[2,128,768]{1,2,0:T(8,128)(2,1)}, u32[]{:S(2)}, u32[]{:S(2)}) collective-permute-start(bf16[2,128,768]{1,2,0:T(8,128)(2,1)} %get-tuple-element.37), channel_id=1, source_target_pairs={{0,4},{4,8},{8,12},{12,16},{16,20},{20,24},{24,28},{28,32},{32,36}... | collective-permute-start | bytes 1179656 | tf_op jit(solution)/shard_map/ppermute | solution.py:18
  140.3 53.2 %collective-permute-start.5 = (bf16[2,128,768]{1,2,0:T(8,128)(2,1)}, bf16[2,128,768]{1,2,0:T(8,128)(2,1)}, u32[]{:S(2)}, u32[]{:S(2)}) collective-permute-start(bf16[2,128,768]{1,2,0:T(8,128)(2,1)} %get-tuple-element.38), channel_id=1, source_target_pairs={{0,124},{4,0},{8,4},{12,8},{16,12},{20,16},{24,20},{28,24},{32,28}... | collective-permute-start | bytes 1179656 | tf_op jit(solution)/shard_map/ppermute | solution.py:18
  145.4 33.5 %collective-permute-start.4 = (bf16[2,128,768]{1,2,0:T(8,128)(2,1)}, bf16[2,128,768]{1,2,0:T(8,128)(2,1)}, u32[]{:S(2)}, u32[]{:S(2)}) collective-permute-start(bf16[2,128,768]{1,2,0:T(8,128)(2,1)} %get-tuple-element.39), channel_id=1, source_target_pairs={{0,120},{4,124},{8,0},{12,4},{16,8},{20,12},{24,16},{28,20},{32,24... | collective-permute-start | bytes 1179656 | tf_op jit(solution)/shard_map/ppermute | solution.py:18
  165.7 6.9 %copy-start.4 = (f32[1024,128]{1,0:T(8,128)S(1)}, f32[1024,128]{1,0:T(8,128)}, u32[]{:S(2)}) copy-start(f32[1024,128]{1,0:T(8,128)} %copy.65) | copy-start | bytes 1572868
  215.8 23.6 %copy-start.10 = (f32[16]{0:T(128)S(1)}, f32[16]{0:T(128)}, u32[]{:S(2)}) copy-start(f32[16]{0:T(128)} %compare_convert_fusion) | copy-start | bytes 196
  240.3 174.6 %all-gather.2.cloned.1.call-start = ((), (), s32[]{:S(2)}) async-start(), calls=%async_computation.1 | async-start | bytes 1474560 | tf_op jit(solution)/shard_map/all_gather | solution.py:137
  393.2 29.5 %copy-start.8 = (f32[48,128]{1,0:T(8,128)S(1)}, f32[48,128]{1,0:T(8,128)}, u32[]{:S(2)}) copy-start(f32[48,128]{1,0:T(8,128)} %copy-done.7) | copy-start | bytes 73732
  (4 other events, 6.7 us)
Sparse Core Ops, SparseCore 0:
  240.4 141.9 all-reduce.1
  392.3 22.6 all-gather.1
where the time goes:
time: 439 us; the launch traced here: 432 us
  waiting for transfers between devices  164 us (37%)
  other arithmetic  129 us (29%)
  local copies, waits for them, and re-layouts  56.3 us (13%)
  matrix products  37 us (8%)
  between operations  31.1 us (7%)
  starting transfers between devices  15.4 us (4%)
    psum x1, waiting for transfers between devices, local(): lax.psum(selector[:, None, None] * local_part[None], ('sub', 'grp'))  142 us
    scatter-add x8, other arithmetic, local(): updated.at[:, dof_idx]  59 us
    scatter-add x4, other arithmetic, local(): updated = updated.at[:, master_idx].add(0.5 * mismatch)  26.1 us
    all_gather x1, waiting for transfers between devices, local(): lax.all_gather(neumann_input, 'grp', axis=1, tiled=True)  21.7 us
    gather x8, local copies, waits for them, and re-layouts, local(): jnp.take(region, master_idx, axis=1)  21.2 us
    dot_general x5, matrix products, contract_last(): lax.dot_general(left_side, right_side, (((1,), (1,)), ((), ())), preferre...  18.8 us
    ppermute x8, starting transfers between devices, passed_along(): return lax.ppermute(value, axis, pairs)  15.3 us
    gather x8, local copies, waits for them, and re-layouts, local(): jnp.take(region, dof_idx, axis=1)  12.8 us
  transfers between devices with their start and end apart: 10, of which 2 were waited for; matrix products, arithmetic and copies ran while one was open for 31% of the time, Pallas kernels for 0%

commit v1 on v0

v1 whole, which is shorter than its diff:
```python
import jax
import jax.numpy as jnp
from jax import lax
from jax.experimental import pallas as pl
from jax.experimental.pallas import tpu as pltpu
from jax.sharding import PartitionSpec as P

FS = 768
FM = 1024
NC = 48
COLS = 128
PAIRS = 4
ROWS = 1152
SUBS = 32
GROUPS = 4
CBLK = 16
REACH = (-2, -1, 1, 2)
HALF = COLS // 2
EXT = FS + 16
F32 = jnp.float32
BF16 = jnp.bfloat16
MESH = pl.DeviceIdType.MESH


def mm_nn(a, b):
    return lax.dot_general(a, b, (((1,), (0,)), ((), ())), preferred_element_type=F32)


def mm_nt(a, b):
    return lax.dot_general(a, b, (((1,), (1,)), ((), ())), preferred_element_type=F32)


def split(x):
    hi = x.astype(BF16)
    return hi, (x - hi.astype(F32)).astype(BF16)


def one_hot(cond):
    return jnp.where(cond, 1.0, 0.0).astype(BF16)


def kernel(
    pair_h, ids_s, res_h, neu_h, proj_h, sdof_h, mdof_h, zb_h, yb_h, cinv_h,
    bal_h, cor_h,
    pair_s, res_v, rbf_v, rin_v, sdof_v, sdin_v, mdof_v, proj_v, u_v, st_v, gt_v,
    neu_v, z_v, y_v, cinv_v, idv_v, idin_v, exp_v, a_v, part_v, m_v, wcat_v, wacc_v,
    base_v, tr_v, mm_v, ret_v, t_v, reply_v, rpin_v, gath_v, acc_v,
    loc_sem, sd_send, sd_recv, rs_send, rs_recv, rp_send, rp_recv,
    id_send, id_recv, pt_send, pt_recv, g_send, g_recv, m_send, m_recv,
):
    s = lax.axis_index("sub")
    g = lax.axis_index("grp")

    def sub_dev(step):
        return (lax.rem(s + step + SUBS, SUBS), g)

    def grp_dev(step):
        return (s, lax.rem(g + step, GROUPS))

    barrier = pltpu.get_barrier_semaphore()

    def greet(r, c):
        pl.semaphore_signal(barrier, inc=1, device_id=sub_dev(r), device_id_type=MESH)
        return c

    lax.fori_loop(1, SUBS, greet, 0)
    for r in range(1, GROUPS):
        pl.semaphore_signal(barrier, inc=1, device_id=grp_dev(r), device_id_type=MESH)

    def local(src, dst, k):
        return pltpu.make_async_copy(src, dst, loc_sem.at[k])

    order = [lax.rem(g + r, GROUPS) for r in (0, 3, 1, 2)]
    cols = [pl.ds(pl.multiple_of(q * ROWS, 128), ROWS) for q in order]
    c_res = local(res_h.at[0], res_v, 0)
    c_sd = local(sdof_h.at[0, 0], sdof_v, 1)
    c_md = local(mdof_h.at[0, 0], mdof_v, 2)
    c_pair = local(pair_h.at[s, g], pair_s, 3)
    c_proj = [local(proj_h.at[0, 0, j], proj_v.at[j, pl.ds(0, FS)], 4 + j) for j in range(PAIRS)]
    c_z = local(zb_h.at[0, :, cols[0]], z_v, 8)
    c_ci = local(cinv_h, cinv_v, 9)
    c_y = [local(yb_h.at[0, :, cols[r]], y_v.at[r], 10 + r) for r in range(GROUPS)]
    c_n = [local(neu_h.at[0, :, cols[r]], neu_v.at[r], 14 + r) for r in range(GROUPS)]
    for c in [c_res, c_sd, c_md, c_pair] + c_proj + [c_z, c_ci] + c_y + c_n:
        c.start()

    idv_v[...] = jnp.full((8, 128), ids_s[0] * NC, jnp.int32)
    idin_v[0] = idv_v[...]
    c_res.wait()
    rbf_v[...] = res_v[...].astype(BF16)
    c_sd.wait()

    pl.semaphore_wait(barrier, SUBS - 1 + GROUPS - 1)

    def rcopy(src, dst, ss, rs, dev):
        return pltpu.make_async_remote_copy(
            src_ref=src, dst_ref=dst, send_sem=ss, recv_sem=rs, device_id=dev, device_id_type=MESH
        )

    sd = [
        rcopy(sdof_v, sdin_v.at[o], sd_send.at[o], sd_recv.at[o], sub_dev(-REACH[o]))
        for o in range(4)
    ]
    rs = [
        rcopy(rbf_v, rin_v.at[o], rs_send.at[o], rs_recv.at[o], sub_dev(-REACH[o]))
        for o in range(4)
    ]
    for o in range(4):
        sd[o].start()
    for o in (0, 3, 1, 2):
        rs[o].start()

    def idc(r):
        return rcopy(idv_v, idin_v.at[r], id_send.at[r], id_recv.at[r], sub_dev(r))

    def id_start(r, c):
        idc(r).start()
        return c

    lax.fori_loop(1, SUBS, id_start, 0)

    c_md.wait()
    for j in range(PAIRS):
        proj_v[j, pl.ds(FS, 16), :] = jnp.ones((16, FM), BF16)
    for j in range(PAIRS):
        c_proj[j].wait()

    def make_u(j, c):
        row = mdof_v[pl.ds(j, 1), :]
        for lo in range(0, ROWS, 256):
            w = min(256, ROWS - lo)
            at = lax.broadcasted_iota(jnp.int32, (w, FM), 0) + lo
            gt_v[pl.ds(0, w), :] = one_hot(at == row)
            u_v[j, :, pl.ds(lo, w)] = mm_nt(proj_v[j], gt_v[pl.ds(0, w), :]).astype(BF16)
        return c

    lax.fori_loop(0, PAIRS, make_u, 0)

    c_pair.wait()
    pos, face = [], []
    for j in range(PAIRS):
        e = lax.rem(pair_s[j, 0] - s + (2 + SUBS), SUBS)
        pos.append(e - lax.div(e, 3))
        face.append(pair_s[j, 1])

    for o in range(4):
        sd[o].wait_recv()
    for j in range(PAIRS):
        code = jnp.full((1, FS), pos[j] * 2 + face[j], jnp.int32)
        row = jnp.zeros((1, FS), jnp.int32)
        for k in range(8):
            row = row + jnp.where(code == k, sdin_v[k // 2, pl.ds(k % 2, 1), :], 0)
        for lo in range(0, ROWS, 128):
            at = lax.broadcasted_iota(jnp.int32, (128, FS), 0) + lo
            st_v[j, pl.ds(lo, 128), :] = one_hot(at == row)

    for o in range(4):
        rs[o].wait_recv()

    base_v[...] = res_v[...]
    for j in range(PAIRS):
        where_j = jnp.full((COLS, ROWS), pos[j], jnp.int32)
        near = rin_v[0] * one_hot(where_j == 0)
        for o in range(1, 4):
            near = near + rin_v[o] * one_hot(where_j == o)
        tr_v[...] = mm_nn(near, st_v[j]).astype(BF16)
        mask = u_v[j, pl.ds(FS, 16), :][0:1, :].astype(F32)
        mism = mm_nn(tr_v[...], u_v[j, pl.ds(0, FS), :]) - mask * res_v[...]
        base_v[...] += 0.5 * mism
        mm_v[...] = mism.astype(BF16)
        ret_v[...] = mm_nt(mm_v[...], u_v[j, pl.ds(0, FS), :]).astype(BF16)
        t_v[j] = mm_nt(ret_v[...], st_v[j])

    rp = [
        rcopy(reply_v.at[o], rpin_v.at[o], rp_send.at[o], rp_recv.at[o], sub_dev(REACH[o]))
        for o in range(4)
    ]
    for o in (0, 3, 1, 2):
        total = jnp.zeros((COLS, ROWS), F32)
        for j in range(PAIRS):
            here = jnp.full((COLS, ROWS), pos[j], jnp.int32) == o
            total = total + jnp.where(here, t_v[j], 0.0)
        reply_v[o] = total.astype(BF16)
        rp[o].start()

    def id_wait(r, c):
        idc(r).wait()
        return c

    lax.fori_loop(1, SUBS, id_wait, 0)
    gap = lax.broadcasted_iota(jnp.int32, (NC, CBLK * NC), 1) - lax.broadcasted_iota(
        jnp.int32, (NC, CBLK * NC), 0
    )

    def make_exp(r, c):
        exp_v[pl.ds(pl.multiple_of(r * NC, 16), NC), :] = one_hot(gap == idin_v[r][0:1, 0:1])
        return c

    lax.fori_loop(0, SUBS, make_exp, 0)
    c_ci.wait()
    my_id = jnp.full((NC, CBLK * NC), ids_s[0], jnp.int32)

    def add_rows(k, rows):
        return rows + jnp.where(my_id == k, cinv_v[pl.ds(pl.multiple_of(k * NC, 8), NC), :], 0.0)

    chi, clo = split(lax.fori_loop(0, CBLK, add_rows, jnp.zeros((NC, CBLK * NC), F32)))
    a_v[...] = mm_nt(jnp.concatenate([chi, clo], 0), exp_v[...]).astype(BF16)

    for r in range(GROUPS):
        c_y[r].wait()
        c_n[r].wait()
        yhi, ylo = split(y_v[r])
        t = mm_nt(jnp.concatenate([yhi, ylo], 0), neu_v[r])
        if r == 0:
            wacc_v[...] = t
        else:
            wacc_v[...] += t
    c_z.wait()
    whi, wlo = split(z_v[...] - wacc_v[0:NC, :] - wacc_v[NC:, :])
    wcat_v[0:NC, :] = whi
    wcat_v[NC : 2 * NC, :] = whi
    wcat_v[2 * NC :, :] = wlo

    for o in range(4):
        rp[o].wait_recv()
        base_v[...] -= 0.5 * rpin_v[o].astype(F32)
    rbf2, rlo2 = split(base_v[...])
    c_bal = local(base_v, bal_h.at[0], 18)
    c_bal.start()
    for o in range(4):
        rs[o].wait_send()
    rbf_v[...] = rbf2

    def half(ref, h):
        return ref.at[pl.ds(h * HALF, HALF)]

    def gcopy(src, slot, h, k, step):
        return rcopy(half(src, h), half(gath_v.at[slot], h), g_send.at[k], g_recv.at[k], grp_dev(step))

    up0 = gcopy(rbf_v, 0, 0, 0, 1)
    dn1 = gcopy(rbf_v, 1, 1, 1, 3)
    up1 = gcopy(rbf_v, 0, 1, 2, 1)
    dn0 = gcopy(rbf_v, 1, 0, 3, 3)
    fup = gcopy(gath_v.at[0], 2, 0, 4, 1)
    fdn = gcopy(gath_v.at[1], 2, 1, 5, 3)
    up0.start()
    dn1.start()
    up1.start()
    dn0.start()

    zhi, zlo = split(z_v[...])
    p2 = mm_nt(jnp.concatenate([zhi, zlo], 0), rbf2)
    part_v[0] = (p2[:NC] + p2[NC:] + mm_nt(zhi, rlo2)).astype(BF16)

    def ptc(r):
        return rcopy(part_v.at[0], part_v.at[r], pt_send.at[r], pt_recv.at[r], sub_dev(r))

    def pt_start(r, c):
        ptc(r).start()
        return c

    lax.fori_loop(1, SUBS, pt_start, 0)
    acc_v[...] = mm_nt(rbf_v[...], neu_v[0])

    up0.wait_recv()
    fup.start()
    dn1.wait_recv()
    fdn.start()

    def pt_wait(r, c):
        ptc(r).wait()
        return c

    lax.fori_loop(1, SUBS, pt_wait, 0)
    parts = part_v[...].reshape(SUBS * NC, COLS)
    m2 = mm_nn(a_v[...], parts)
    m_v[0] = m2[:NC] + m2[NC:]

    mc = [rcopy(m_v.at[0], m_v.at[r], m_send.at[r], m_recv.at[r], grp_dev(r)) for r in range(1, 4)]
    for c in mc:
        c.start()

    up1.wait_recv()
    acc_v[...] += mm_nt(gath_v[0], neu_v[1])
    dn0.wait_recv()
    acc_v[...] += mm_nt(gath_v[1], neu_v[2])
    for c in mc:
        c.wait()
    mhi, mlo = split((m_v[0] + m_v[1] + m_v[2] + m_v[3]).T)
    mcat = jnp.concatenate([mhi, mlo, mhi], 1)
    acc_v[...] += mm_nn(mcat, wcat_v[...])
    fup.wait_recv()
    fdn.wait_recv()
    acc_v[...] += mm_nt(gath_v[2], neu_v[3])
    c_cor = local(acc_v, cor_h.at[0], 19)
    c_cor.start()
    for c in sd + rp + [up0, dn1, up1, dn0, fup, fdn]:
        c.wait_send()
    c_bal.wait()
    c_cor.wait()


def local_part(
    residual, neumann, projection, pair_list, slave_dofs, master_dofs, zbasis, ybasis, coarse_inverse, coarse_ids
):
    any_spec = pl.BlockSpec(memory_space=pl.ANY)
    smem_spec = pl.BlockSpec(memory_space=pltpu.SMEM)
    dma = pltpu.SemaphoreType.DMA
    vm = pltpu.VMEM
    region = jax.ShapeDtypeStruct((1, COLS, ROWS), F32)
    scratch = [
        pltpu.SMEM((PAIRS, 2), jnp.int32),
        vm((COLS, ROWS), F32),
        vm((COLS, ROWS), BF16),
        vm((4, COLS, ROWS), BF16),
        vm((2, FS), jnp.int32),
        vm((4, 2, FS), jnp.int32),
        vm((PAIRS, FM), jnp.int32),
        vm((PAIRS, EXT, FM), BF16),
        vm((PAIRS, EXT, ROWS), BF16),
        vm((PAIRS, ROWS, FS), BF16),
        vm((256, FM), BF16),
        vm((GROUPS, ROWS, ROWS), BF16),
        vm((NC, ROWS), F32),
        vm((GROUPS, NC, ROWS), F32),
        vm((CBLK * NC, CBLK * NC), F32),
        vm((8, 128), jnp.int32),
        vm((SUBS, 8, 128), jnp.int32),
        vm((SUBS * NC, CBLK * NC), BF16),
        vm((2 * NC, SUBS * NC), BF16),
        vm((SUBS, NC, COLS), BF16),
        vm((GROUPS, NC, COLS), F32),
        vm((3 * NC, ROWS), BF16),
        vm((2 * NC, ROWS), F32),
        vm((COLS, ROWS), F32),
        vm((COLS, FS), BF16),
        vm((COLS, ROWS), BF16),
        vm((COLS, FS), BF16),
        vm((PAIRS, COLS, ROWS), F32),
        vm((4, COLS, ROWS), BF16),
        vm((4, COLS, ROWS), BF16),
        vm((3, COLS, ROWS), BF16),
        vm((COLS, ROWS), F32),
        dma((20,)),
        dma((4,)), dma((4,)), dma((4,)), dma((4,)), dma((4,)), dma((4,)),
        dma((SUBS,)), dma((SUBS,)), dma((SUBS,)), dma((SUBS,)),
        dma((6,)), dma((6,)), dma((4,)), dma((4,)),
    ]
    return pl.pallas_call(
        kernel,
        out_shape=(region, region),
        in_specs=[any_spec, smem_spec] + [any_spec] * 8,
        out_specs=(any_spec, any_spec),
        scratch_shapes=scratch,
        compiler_params=pltpu.CompilerParams(
            collective_id=0, has_side_effects=True, vmem_limit_bytes=60 * 1024 * 1024
        ),
    )(
        pair_list, coarse_ids, residual, neumann, projection, slave_dofs, master_dofs, zbasis, ybasis, coarse_inverse
    )


def solution(mesh):
    placed = (
        P("sub", None, "grp"),
        P("sub", "grp", None),
        P("sub", "grp", None, None, None),
        P(),
        P("sub", "grp", None, None),
        P("sub", "grp", None, None),
        P("sub", None, None),
        P("sub", None, None),
        P(),
        P("sub"),
    )
    return jax.shard_map(
        local_part,
        mesh=mesh,
        in_specs=placed,
        out_specs=(P("sub", None, "grp"), P("sub", None, "grp")),
        check_vma=False,
    )
```

time: 439 us -> 63.2 us (0.14); the launches traced: 432 us -> 62.9 us
  waiting for transfers between devices: 164 us -> 0 us
  other arithmetic: 129 us -> 0 us
  Pallas kernels: 0 us -> 56.2 us
  local copies, waits for them, and re-layouts: 56.3 us -> 5.43 us
  matrix products: 37 us -> 0 us
  between operations: 31.1 us -> 1.29 us
  starting transfers between devices: 15.4 us -> 0 us
    psum x1 -> x0, waiting for transfers between devices: 142 us -> none  [local(): lax.psum(selector[:, None, None] * local_part[None], ('sub', 'grp'))]
    scatter-add x12 -> x0, other arithmetic: 85.1 us -> none  [the longest x8 59 us: local(): updated.at[:, dof_idx]]
    pallas_call x0 -> x1, Pallas kernels: none -> 56.2 us  [local_part(): pl.pallas_call(kernel, out_shape=(region, region), in_specs=[any_spec, sm...]
    dot_general x13 -> x0, matrix products: 37 us -> none  [the longest x5 18.8 us: contract_last(): lax.dot_general(left_side, right_side, (((1,), (1,)), ((), ())), preferre...]
    gather x16 -> x0, local copies, waits for them, and re-layouts: 34 us -> none  [the longest x8 21.2 us: local(): jnp.take(region, master_idx, axis=1)]
    all_gather x1 -> x0, waiting for transfers between devices: 21.7 us -> none  [local(): lax.all_gather(neumann_input, 'grp', axis=1, tiled=True)]
    ppermute x8 -> x0, starting transfers between devices: 15.3 us -> none  [passed_along(): return lax.ppermute(value, axis, pairs)]
    eq x21 -> x0, other arithmetic: 14.7 us -> none  [the longest x8 5.16 us: local(): jnp.arange(SFACES)[:, None] == face_id]
  transfers between devices with their start and end apart: 10 -> 0, of which waited for: 2 -> 0; matrix products, arithmetic and copies ran while one was open for 31% -> 0% of each run, Pallas kernels for 0% -> 0%
where the time goes in v1:
time: 63.2 us; the launch traced here: 62.9 us
  Pallas kernels  56.2 us (89%)
  local copies, waits for them, and re-layouts  5.43 us (9%)
  between operations  1.29 us (2%)
    pallas_call x1, Pallas kernels, local_part(): pl.pallas_call(kernel, out_shape=(region, region), in_specs=[any_spec, sm...  56.2 us
    unnamed x3, local copies, waits for them, and re-layouts  5.43 us

profile of v1, /device:TPU:0, one launch (start us, length us, event | category | flops | bytes accessed | tf_op | source)
XLA Modules:
  0.0 62.9 jit_solution(5196564496110811635)
XLA Ops:
  1.3 1.6 %copy.12.pair_h = s32[32,4,4,2]{3,2,1,0:T(4,128)} copy(s32[32,4,4,2]{0,3,2,1:T(2,128)} %param.13) | data formatting | bytes 8192 | tf_op args[3]
  2.9 56.2 %shard_map.113 = (f32[1,128,1152]{2,1,0:T(8,128)}, f32[1,128,1152]{2,1,0:T(8,128)}) custom-call(s32[32,4,4,2]{3,2,1,0:T(4,128)} %copy.12.pair_h, s32[1]{0:T(128)S(6)} %copy.15.ids_s, f32[1,128,1152]{2,1,0:T(8,128)} %res_h.1, bf16[1,1152,4608]{2,1,0:T(8,128)(2,1)} %neu_h.1, bf16[1,1,4,768,1024]{4,3,2,1,0:T(8,128)(2,1)} %proj_h.1, s32[1,1,2,768]{3,2,1,0:T(2,128)} %sdof_h.1, ...), custom_call_target="tpu_custom_call" | custom-call | tf_op jit(solution)/shard_map/pallas_call | solution.py:349
  59.1 1.9 %copy.16 = f32[1,128,1152]{2,1,0:T(8,128)} copy(f32[1,128,1152]{2,1,0:T(8,128)} %get-tuple-element.4) | data formatting | bytes 1179648
  61.0 1.9 %copy.17 = f32[1,128,1152]{2,1,0:T(8,128)} copy(f32[1,128,1152]{2,1,0:T(8,128)} %get-tuple-element.5) | data formatting | bytes 1179648

commit v2 on v1

v2 whole, which is shorter than its diff:
```python
import jax
import jax.numpy as jnp
from jax import lax
from jax.experimental import pallas as pl
from jax.experimental.pallas import tpu as pltpu
from jax.sharding import PartitionSpec as P

FS = 768
FM = 1024
NC = 48
COLS = 128
PAIRS = 4
ROWS = 1152
SUBS = 32
GROUPS = 4
CBLK = 16
REACH = (-2, -1, 1, 2)
HALF = COLS // 2
CHUNKS = 3
CW = ROWS // CHUNKS
ROW = 8
PLANES = SUBS // ROW
CHIPS = SUBS // 2
F32 = jnp.float32
BF16 = jnp.bfloat16
I32 = jnp.int32
MESH = pl.DeviceIdType.MESH


def mm_nn(a, b):
    return lax.dot_general(a, b, (((1,), (0,)), ((), ())), preferred_element_type=F32)


def mm_nt(a, b):
    return lax.dot_general(a, b, (((1,), (1,)), ((), ())), preferred_element_type=F32)


def split(x):
    hi = x.astype(BF16)
    return hi, (x - hi.astype(F32)).astype(BF16)


def one_hot(cond):
    return jnp.where(cond, 1.0, 0.0).astype(BF16)


def kernel(
    pair_h, ids_s, res_h, neu_h, proj_h, sdof_h, mdof_h, zb_h, yb_h, cinv_h,
    bal_h, cor_h,
    pair_v, res_v, rbf_v, lhs_v, rin_v, sdof_v, sdin_v, mdof_v, proj_v, gt_v, rg_v, zg_v, st_v,
    zsf_v, zsin_v, neu_v, z_v, y_v, cinv_v, idrow_v, idcol_v, ecol_v, erow_v, t1_v, a_v,
    c_v, cin_v, col_v, pxo_v, pxi_v, m_v, wcat_v, wacc_v, w32_v, w16_v, v32_v, v16_v,
    base_v, part_v, tr_v, mm_v, ret_v, t_v, ab32_v, ab_v, cd_v, sw_v, sum_v, rpin_v, bal_v, gath_v, acc_v,
    loc_sem, sd_send, sd_recv, zs_send, zs_recv, c_send, c_recv, p1_send, p1_recv, fw_send, fw_recv,
    sw_send, sw_recv, cd_send, cd_recv, ab_send, ab_recv,
    ix_send, ix_recv, iz_send, iz_recv, px_send, px_recv, pz_send, pz_recv,
    g_send, g_recv, m_send, m_recv,
):
    s = lax.axis_index("sub")
    g = lax.axis_index("grp")
    core = lax.rem(s, 2)
    chip = lax.div(s, 2)
    row = lax.rem(s, ROW)

    def sub_dev(step):
        return (lax.rem(s + step + SUBS, SUBS), g)

    def chip_dev(step, c):
        return (lax.rem(chip + step + CHIPS, CHIPS) * 2 + c, g)

    def row_dev(r):
        return (s - row + lax.rem(row + r, ROW), g)

    def grp_dev(step):
        return (s, lax.rem(g + step, GROUPS))

    mate = (s + 1 - 2 * core, g)

    barrier = pltpu.get_barrier_semaphore()
    greeted = [sub_dev(k) for k in REACH] + [row_dev(r) for r in range(1, ROW)]
    greeted += [sub_dev(ROW * k) for k in range(1, PLANES)] + [grp_dev(k) for k in range(1, GROUPS)]
    for dev in greeted:
        pl.semaphore_signal(barrier, inc=1, device_id=dev, device_id_type=MESH)

    def local(src, dst, k):
        return pltpu.make_async_copy(src, dst, loc_sem.at[k])

    order = [lax.rem(g + r, GROUPS) for r in (0, 3, 1, 2)]
    cols = [pl.ds(pl.multiple_of(q * ROWS, 128), ROWS) for q in order]
    c_res = local(res_h.at[0], res_v, 0)
    c_sd = local(sdof_h.at[0, 0], sdof_v, 1)
    c_md = local(mdof_h.at[0, 0], mdof_v, 2)
    c_pair = local(pair_h.at[g], pair_v, 3)
    c_proj = [local(proj_h.at[0, 0, j], proj_v.at[j], 4 + j) for j in range(PAIRS)]
    c_z = local(zb_h.at[0, :, cols[0]], z_v, 8)
    c_ci = local(cinv_h, cinv_v, 9)
    c_y = [local(yb_h.at[0, :, cols[r]], y_v.at[r], 10 + r) for r in range(GROUPS)]
    c_n = [local(neu_h.at[0, :, cols[r]], neu_v.at[r], 14 + r) for r in range(GROUPS)]
    for c in [c_res, c_sd, c_md, c_pair, c_z] + c_proj + [c_ci] + c_y + c_n:
        c.start()

    idrow_v[0] = jnp.full((8, 128), ids_s[0] * NC, I32)
    idcol_v[0] = idrow_v[0]
    c_res.wait()
    rbf_v[...] = res_v[...].astype(BF16)
    c_sd.wait()

    pl.semaphore_wait(barrier, len(greeted))

    def rcopy(src, dst, ss, rs, dev):
        return pltpu.make_async_remote_copy(
            src_ref=src, dst_ref=dst, send_sem=ss, recv_sem=rs, device_id=dev, device_id_type=MESH
        )

    def half(ref, h):
        return ref.at[pl.ds(pl.multiple_of(h * HALF, HALF), HALF)]

    sd = [
        rcopy(sdof_v, sdin_v.at[o], sd_send.at[o], sd_recv.at[o], sub_dev(-REACH[o]))
        for o in range(4)
    ]
    shared_step = 2 * core - 1
    p1 = [
        rcopy(half(rbf_v, h), half(rin_v.at[1 - core], h), p1_send.at[h], p1_recv.at[1 - core],
              chip_dev(shared_step, h))
        for h in range(2)
    ]
    p1.append(rcopy(rbf_v, rin_v.at[2], p1_send.at[2], p1_recv.at[2], chip_dev(-shared_step, core)))
    p1.append(rcopy(rbf_v, rin_v.at[3], p1_send.at[3], p1_recv.at[3], mate))
    for c in sd + p1:
        c.start()

    ix = [rcopy(idrow_v.at[0], idrow_v.at[r], ix_send.at[r], ix_recv.at[r], row_dev(r)) for r in range(1, ROW)]
    iz = [
        rcopy(idcol_v.at[0], idcol_v.at[k], iz_send.at[k], iz_recv.at[k], sub_dev(ROW * k))
        for k in range(1, PLANES)
    ]
    for c in ix + iz:
        c.start()

    c_z.wait()
    zhi, zlo = split(z_v[...])
    lhs_v[0:COLS, :] = rbf_v[...]
    lhs_v[COLS : 2 * COLS, :] = (res_v[...] - rbf_v[...].astype(F32)).astype(BF16)
    lhs_v[2 * COLS : 2 * COLS + NC, :] = zhi
    lhs_v[2 * COLS + NC :, :] = zlo
    at_face = lax.broadcasted_iota(I32, (ROWS, FS), 0)
    for f in range(2):
        st_v[f] = one_hot(at_face == sdof_v[pl.ds(f, 1), :])
        zsf_v[f] = mm_nn(lhs_v[2 * COLS : 2 * COLS + NC, :], st_v[f]).astype(BF16)
    zs = [
        rcopy(zsf_v, zsin_v.at[o], zs_send.at[o], zs_recv.at[o], sub_dev(-REACH[o])) for o in range(4)
    ]
    for c in zs:
        c.start()

    c_pair.wait()
    lane = lax.broadcasted_iota(I32, (1, SUBS), 1)

    def entry(j, k):
        line = pair_v[j, pl.ds(k, 1), :].astype(F32)
        return jnp.sum(jnp.where(lane == s, line, 0.0), axis=1, keepdims=True).astype(I32)

    near = [(entry(j, 0) - s + (SUBS + 2)) & (SUBS - 1) for j in range(PAIRS)]
    face = [entry(j, 1) for j in range(PAIRS)]
    slot_e = [1 - core, 4 - core, 4 * core, 3 - 2 * core]
    for j in range(PAIRS):
        here = jnp.broadcast_to(near[j], (16, 128))
        side = jnp.broadcast_to(face[j], (16, 128))
        for q in range(4):
            hot = jnp.where(here == slot_e[q], 1.0, 0.0)
            w32_v[j, q] = hot[0:8]
            w16_v[j, q] = hot.astype(BF16)
            hot = jnp.where(here == REACH[q] + 2, 1.0, 0.0)
            v32_v[j, q] = hot[0:8]
            for k in range(2):
                v16_v[j, q, k] = jnp.where(side == k, hot, 0.0).astype(BF16)

    c_md.wait()

    def make_g(j, c):
        line = mdof_v[pl.ds(j, 1), :]
        gt_v[j] = one_hot(lax.broadcasted_iota(I32, (ROWS, FM), 0) == line)
        for lo in range(0, FM, 256):
            w = pl.ds(lo, 256)
            got = mm_nn(lhs_v[...], gt_v[j, :, w])
            rg_v[j, :, w] = got[0:COLS] + got[COLS : 2 * COLS]
            zg_v[j, :, w] = got[2 * COLS :].astype(BF16)
        return c

    lax.fori_loop(0, PAIRS, make_g, 0)
    res_part = mm_nt(lhs_v[2 * COLS :, :], rbf_v[...])
    part_v[...] = res_part[:NC] + res_part[NC:] + mm_nt(
        lhs_v[2 * COLS : 2 * COLS + NC, :], lhs_v[COLS : 2 * COLS, :]
    )

    for c in sd:
        c.wait_recv()
    for j in range(PAIRS):
        code = jnp.broadcast_to(near[j] * 2 + face[j], (1, FS))
        line = jnp.zeros((1, FS), I32)
        for o in range(4):
            for k in range(2):
                line = line + jnp.where(code == (REACH[o] + 2) * 2 + k, sdin_v[o, pl.ds(k, 1), :], 0)
        st_v[j] = one_hot(at_face == line)

    for c in ix + iz:
        c.wait()
    gap = lax.broadcasted_iota(I32, (NC, CBLK * NC), 1) - lax.broadcasted_iota(I32, (NC, CBLK * NC), 0)
    for k in range(PLANES):
        ecol_v[k * NC : (k + 1) * NC, :] = one_hot(gap == idcol_v[k][0:1, 0:1])
    for r in range(ROW):
        erow_v[r * NC : (r + 1) * NC, :] = one_hot(gap == idrow_v[(ROW - r) % ROW][0:1, 0:1])
    c_ci.wait()
    chi, clo = split(cinv_v[...])
    t1_v[0] = mm_nt(chi, ecol_v[...]).astype(BF16)
    t1_v[1] = mm_nt(clo, ecol_v[...]).astype(BF16)
    for k in range(2):
        a_v[k] = mm_nn(erow_v[...], t1_v[k]).astype(BF16)

    fw = [
        rcopy(half(rin_v.at[q], core), half(rin_v.at[q], core), fw_send.at[q], fw_recv.at[q], mate)
        for q in range(2)
    ]
    got = [
        rcopy(half(rbf_v, 0), half(rin_v.at[q], core), p1_send.at[0], p1_recv.at[q], mate) for q in range(2)
    ]
    for q in range(2):
        got[q].wait_recv()
        fw[q].start()
    for c in c_proj:
        c.wait()
    p1[2].wait_recv()
    p1[3].wait_recv()
    for q in range(2):
        fw[q].wait_recv()

    for j in range(PAIRS):
        there = rin_v[0] * jnp.tile(w16_v[j, 0], (8, 9))
        for q in range(1, 4):
            there = there + rin_v[q] * jnp.tile(w16_v[j, q], (8, 9))
        tr_v[j] = mm_nn(there, st_v[j]).astype(BF16)
    for j in range(PAIRS):
        mhi, mlo = split(mm_nn(tr_v[j], proj_v[j]) - rg_v[j])
        mm_v[j, 0:COLS, :] = mhi
        mm_v[j, COLS:, :] = mlo
        ret_v[j] = mm_nt(mhi, proj_v[j]).astype(BF16)

    for c in zs:
        c.wait_recv()
    cc = [rcopy(c_v.at[o], cin_v.at[o], c_send.at[o], c_recv.at[o], sub_dev(REACH[o])) for o in range(4)]
    shares = []
    for j in range(PAIRS):
        zsel = jnp.zeros((NC, FS), BF16)
        for o in range(4):
            for k in range(2):
                zsel = zsel + zsin_v[o, k] * jnp.tile(v16_v[j, o, k], (3, 6))
        shares.append(mm_nt(zsel, ret_v[j]))
    for o in range(4):
        total = shares[0] * jnp.tile(v32_v[0, o], (6, 1))
        for j in range(1, PAIRS):
            total = total + shares[j] * jnp.tile(v32_v[j, o], (6, 1))
        c_v[o] = (-0.5 * total).astype(BF16)
        cc[o].start()

    swc, cdc, abc = [], [], []
    for ch in range(CHUNKS):
        swc.append(rcopy(ab_v.at[ch, 1 - core], sw_v.at[ch], sw_send.at[ch], sw_recv.at[ch], mate))
        cdc.append([
            rcopy(cd_v.at[ch, 0], rpin_v.at[1, ch], cd_send.at[ch, 0], cd_recv.at[ch, 0],
                  chip_dev(shared_step, core)),
            rcopy(cd_v.at[ch, 1], rpin_v.at[2, ch], cd_send.at[ch, 1], cd_recv.at[ch, 1], mate),
        ])
        abc.append([
            rcopy(sum_v.at[ch, q], half(rpin_v.at[0, ch], core), ab_send.at[ch, q], ab_recv.at[ch, core],
                  chip_dev(2 * q - 1, 1 - q))
            for q in range(2)
        ])

    def add_swapped(ch):
        swc[ch].wait_recv()
        for q in range(2):
            mine = ab32_v[ch, q, pl.ds(pl.multiple_of(core * HALF, HALF), HALF), :]
            sum_v[ch, q] = (mine + sw_v[ch, q].astype(F32)).astype(BF16)
            abc[ch][q].start()

    for ch in range(CHUNKS):
        for j in range(PAIRS):
            t_v[j] = mm_nt(ret_v[j], st_v[j, pl.ds(ch * CW, CW), :])
        for q in range(4):
            total = t_v[0] * jnp.tile(w32_v[0, q], (16, 3))
            for j in range(1, PAIRS):
                total = total + t_v[j] * jnp.tile(w32_v[j, q], (16, 3))
            if q < 2:
                ab32_v[ch, q] = total
                for h in range(2):
                    ab_v[ch, h, q] = total[h * HALF : (h + 1) * HALF].astype(BF16)
            else:
                cd_v[ch, q - 2] = total.astype(BF16)
            if q == 1:
                swc[ch].start()
        cdc[ch][0].start()
        cdc[ch][1].start()
        if ch > 0:
            add_swapped(ch - 1)
    add_swapped(CHUNKS - 1)

    def scatter(ch):
        at = pl.ds(ch * CW, CW)
        moved = mm_nt(mm_v[0], gt_v[0, at, :])
        for j in range(1, PAIRS):
            moved = moved + mm_nt(mm_v[j], gt_v[j, at, :])
        base_v[:, at] = res_v[:, at] + 0.5 * (moved[:COLS] + moved[COLS:])

    scatter(0)

    part = jnp.zeros((2 * NC, 2 * COLS), F32)
    for j in range(PAIRS):
        part = part + mm_nt(zg_v[j], mm_v[j])
    part = part_v[...] + 0.5 * (part[:NC, :COLS] + part[NC:, :COLS] + part[:NC, COLS:])
    for o in range(4):
        cc[o].wait_recv()
        part = part + cin_v[o].astype(F32)
    col_v[0] = part.astype(BF16)
    pz = [
        rcopy(col_v.at[0], col_v.at[k], pz_send.at[k], pz_recv.at[k], sub_dev(ROW * k))
        for k in range(1, PLANES)
    ]
    for c in pz:
        c.start()

    def gcopy(src, ch, slot, h, k, step):
        return rcopy(half(src, h), half(gath_v.at[slot, ch], h), g_send.at[ch, k], g_recv.at[ch, k], grp_dev(step))

    gat = []
    for ch in range(CHUNKS):
        gat.append([
            gcopy(bal_v.at[ch], ch, 0, 0, 0, 1),
            gcopy(bal_v.at[ch], ch, 1, 1, 1, 3),
            gcopy(bal_v.at[ch], ch, 0, 1, 2, 1),
            gcopy(bal_v.at[ch], ch, 1, 0, 3, 3),
            gcopy(gath_v.at[0, ch], ch, 2, 0, 4, 1),
            gcopy(gath_v.at[1, ch], ch, 2, 1, 5, 3),
        ])

    def balance(ch):
        at = pl.ds(ch * CW, CW)
        cdc[ch][0].wait_recv()
        cdc[ch][1].wait_recv()
        for h in range(2):
            rcopy(sum_v.at[ch, 0], half(rpin_v.at[0, ch], h), ab_send.at[ch, 0], ab_recv.at[ch, h], mate).wait_recv()
        back = rpin_v[0, ch].astype(F32) + rpin_v[1, ch].astype(F32) + rpin_v[2, ch].astype(F32)
        new = base_v[:, at] - 0.5 * back
        base_v[:, at] = new
        bal_v[ch] = new.astype(BF16)
        for k in range(4):
            gat[ch][k].start()

    def forward(ch):
        gat[ch][0].wait_recv()
        gat[ch][4].start()
        gat[ch][1].wait_recv()
        gat[ch][5].start()

    def solve(block, ch, x):
        return mm_nt(x, neu_v[block, :, pl.ds(ch * CW, CW)])

    balance(0)
    scatter(1)
    balance(1)
    scatter(2)

    for c in pz:
        c.wait()
    column = col_v[...].reshape(PLANES * NC, COLS)
    made = (mm_nn(a_v[0], column) + mm_nn(a_v[1], column)).astype(BF16)
    for r in range(ROW):
        pxo_v[r] = made[r * NC : (r + 1) * NC]
    px = [rcopy(pxo_v.at[r], pxi_v.at[r], px_send.at[r], px_recv.at[r], row_dev(r)) for r in range(1, ROW)]
    for c in px:
        c.start()
    balance(2)
    c_bal = local(base_v, bal_h.at[0], 18)
    c_bal.start()

    for r in range(GROUPS):
        c_y[r].wait()
        c_n[r].wait()
        yhi, ylo = split(y_v[r])
        t = mm_nt(jnp.concatenate([yhi, ylo], 0), neu_v[r])
        if r == 0:
            wacc_v[...] = t
        else:
            wacc_v[...] += t
    whi, wlo = split(z_v[...] - wacc_v[0:NC, :] - wacc_v[NC:, :])
    wcat_v[0:NC, :] = whi
    wcat_v[NC : 2 * NC, :] = whi
    wcat_v[2 * NC :, :] = wlo

    forward(0)
    forward(1)
    mine = pxo_v[0].astype(F32)
    for r in range(1, ROW):
        px[r - 1].wait()
        mine = mine + pxi_v[r].astype(F32)
    m_v[0] = mine
    mc = [rcopy(m_v.at[0], m_v.at[r], m_send.at[r], m_recv.at[r], grp_dev(r)) for r in range(1, 4)]
    for c in mc:
        c.start()
    acc_v[...] = solve(0, 0, bal_v[0])
    acc_v[...] += solve(0, 1, bal_v[1])
    forward(2)
    acc_v[...] += solve(0, 2, bal_v[2])
    for ch in range(CHUNKS):
        for q in range(2):
            gat[ch][2 + q].wait_recv()
            acc_v[...] += solve(1 + q, ch, gath_v[q, ch])
    for c in mc:
        c.wait()
    mhi, mlo = split((m_v[0] + m_v[1] + m_v[2] + m_v[3]).T)
    acc_v[...] += mm_nn(jnp.concatenate([mhi, mlo, mhi], 1), wcat_v[...])
    for ch in range(CHUNKS):
        gat[ch][4].wait_recv()
        gat[ch][5].wait_recv()
        acc_v[...] += solve(3, ch, gath_v[2, ch])
    c_cor = local(acc_v, cor_h.at[0], 19)
    c_cor.start()
    for c in sd + zs + cc + p1 + fw + swc:
        c.wait_send()
    for ch in range(CHUNKS):
        for c in cdc[ch] + abc[ch] + gat[ch]:
            c.wait_send()
    c_bal.wait()
    c_cor.wait()


def hand_over(a_ref, b_ref, x_ref, y_ref):
    x_ref[...] = a_ref[...]
    y_ref[...] = b_ref[...]


def local_part(
    residual, neumann, projection, pair_list, slave_dofs, master_dofs, zbasis, ybasis, coarse_inverse, coarse_ids
):
    any_spec = pl.BlockSpec(memory_space=pl.ANY)
    smem_spec = pl.BlockSpec(memory_space=pltpu.SMEM)
    dma = pltpu.SemaphoreType.DMA
    vm = pltpu.VMEM
    region = jax.ShapeDtypeStruct((1, COLS, ROWS), F32)
    scratch = [
        vm((PAIRS, 2, SUBS), I32),
        vm((COLS, ROWS), F32),
        vm((COLS, ROWS), BF16),
        vm((2 * COLS + 2 * NC, ROWS), BF16),
        vm((4, COLS, ROWS), BF16),
        vm((2, FS), I32),
        vm((4, 2, FS), I32),
        vm((PAIRS, FM), I32),
        vm((PAIRS, FS, FM), BF16),
        vm((PAIRS, ROWS, FM), BF16),
        vm((PAIRS, COLS, FM), F32),
        vm((PAIRS, 2 * NC, FM), BF16),
        vm((PAIRS, ROWS, FS), BF16),
        vm((2, NC, FS), BF16),
        vm((4, 2, NC, FS), BF16),
        vm((GROUPS, ROWS, ROWS), BF16),
        vm((NC, ROWS), F32),
        vm((GROUPS, NC, ROWS), F32),
        vm((CBLK * NC, CBLK * NC), F32),
        vm((ROW, 8, 128), I32),
        vm((PLANES, 8, 128), I32),
        vm((PLANES * NC, CBLK * NC), BF16),
        vm((ROW * NC, CBLK * NC), BF16),
        vm((2, CBLK * NC, PLANES * NC), BF16),
        vm((2, ROW * NC, PLANES * NC), BF16),
        vm((4, NC, COLS), BF16),
        vm((4, NC, COLS), BF16),
        vm((PLANES, NC, COLS), BF16),
        vm((ROW, NC, COLS), BF16),
        vm((ROW, NC, COLS), BF16),
        vm((GROUPS, NC, COLS), F32),
        vm((3 * NC, ROWS), BF16),
        vm((2 * NC, ROWS), F32),
        vm((PAIRS, 4, 8, 128), F32),
        vm((PAIRS, 4, 16, 128), BF16),
        vm((PAIRS, 4, 8, 128), F32),
        vm((PAIRS, 4, 2, 16, 128), BF16),
        vm((COLS, ROWS), F32),
        vm((NC, COLS), F32),
        vm((PAIRS, COLS, FS), BF16),
        vm((PAIRS, 2 * COLS, FM), BF16),
        vm((PAIRS, COLS, FS), BF16),
        vm((PAIRS, COLS, CW), F32),
        vm((CHUNKS, 2, COLS, CW), F32),
        vm((CHUNKS, 2, 2, HALF, CW), BF16),
        vm((CHUNKS, 2, COLS, CW), BF16),
        vm((CHUNKS, 2, HALF, CW), BF16),
        vm((CHUNKS, 2, HALF, CW), BF16),
        vm((3, CHUNKS, COLS, CW), BF16),
        vm((CHUNKS, COLS, CW), BF16),
        vm((3, CHUNKS, COLS, CW), BF16),
        vm((COLS, ROWS), F32),
        dma((20,)),
        dma((4,)), dma((4,)), dma((4,)), dma((4,)), dma((4,)), dma((4,)),
        dma((4,)), dma((4,)), dma((2,)), dma((2,)),
        dma((CHUNKS,)), dma((CHUNKS,)), dma((CHUNKS, 2)), dma((CHUNKS, 2)), dma((CHUNKS, 2)), dma((CHUNKS, 2)),
        dma((ROW,)), dma((ROW,)), dma((PLANES,)), dma((PLANES,)),
        dma((ROW,)), dma((ROW,)), dma((PLANES,)), dma((PLANES,)),
        dma((CHUNKS, 6)), dma((CHUNKS, 6)), dma((4,)), dma((4,)),
    ]
    outs = pl.pallas_call(
        kernel,
        out_shape=(region, region),
        in_specs=[any_spec, smem_spec] + [any_spec] * 8,
        out_specs=(any_spec, any_spec),
        scratch_shapes=scratch,
        compiler_params=pltpu.CompilerParams(
            collective_id=0, has_side_effects=True, vmem_limit_bytes=60 * 1024 * 1024
        ),
    )(
        jnp.transpose(pair_list, (1, 2, 3, 0)), coarse_ids, residual, neumann, projection,
        slave_dofs, master_dofs, zbasis, ybasis, coarse_inverse,
    )
    whole = pl.BlockSpec(memory_space=pltpu.VMEM)
    return pl.pallas_call(
        hand_over,
        out_shape=(region, region),
        in_specs=[whole, whole],
        out_specs=(whole, whole),
    )(*outs)


def solution(mesh):
    placed = (
        P("sub", None, "grp"),
        P("sub", "grp", None),
        P("sub", "grp", None, None, None),
        P(),
        P("sub", "grp", None, None),
        P("sub", "grp", None, None),
        P("sub", None, None),
        P("sub", None, None),
        P(),
        P("sub"),
    )
    return jax.shard_map(
        local_part,
        mesh=mesh,
        in_specs=placed,
        out_specs=(P("sub", None, "grp"), P("sub", None, "grp")),
        check_vma=False,
    )
```

time: 63.2 us -> 57.4 us (0.908)
  local copies, waits for them, and re-layouts: 5.43 us -> 0 us
    unnamed x3 -> x0, local copies, waits for them, and re-layouts: 5.43 us -> none
    pallas_call x1, Pallas kernels: 56.2 us -> 53.7 us  [local_part(): pl.pallas_call(kernel, out_shape=(region, region), in_specs=[any_spec, sm...]
    pallas_call x0 -> x1, Pallas kernels: none -> 2.29 us  [local_part(): pl.pallas_call(hand_over, out_shape=(region, region), in_specs=[whole, wh...]
where the time goes in v2:
time: 57.4 us; the launch traced here: 57.3 us
  Pallas kernels  56 us (98%)
  between operations  1.29 us (2%)
    pallas_call x1, Pallas kernels, local_part(): pl.pallas_call(kernel, out_shape=(region, region), in_specs=[any_spec, sm...  53.7 us
    pallas_call x1, Pallas kernels, local_part(): pl.pallas_call(hand_over, out_shape=(region, region), in_specs=[whole, wh...  2.29 us

profile of v2, /device:TPU:0, one launch (start us, length us, event | category | flops | bytes accessed | tf_op | source)
XLA Modules:
  0.0 57.3 jit_solution(13249249034431489019)
XLA Ops:
  1.3 53.7 %shard_map.113 = (f32[1,128,1152]{2,1,0:T(8,128)}, f32[1,128,1152]{2,1,0:T(8,128)}) custom-call(s32[4,4,2,32]{3,2,1,0:T(2,128)} %bitcast.1, s32[1]{0:T(128)S(6)} %copy.12.ids_s, f32[1,128,1152]{2,1,0:T(8,128)} %res_h.1, bf16[1,1152,4608]{2,1,0:T(8,128)(2,1)} %neu_h.1, bf16[1,1,4,768,1024]{4,3,2,1,0:T(8,128)(2,1)} %proj_h.1, s32[1,1,2,768]{3,2,1,0:T(2,128)} %sdof_h.1, ...), custom_call_target="tpu_custom_call" | custom-call | tf_op jit(solution)/shard_map/pallas_call | solution.py:511
  55.0 2.3 %shard_map.114 = (f32[1,128,1152]{2,1,0:T(8,128)}, f32[1,128,1152]{2,1,0:T(8,128)}) custom-call(f32[1,128,1152]{2,1,0:T(8,128)} %get-tuple-element.4.a_ref, f32[1,128,1152]{2,1,0:T(8,128)} %get-tuple-element.5.b_ref), custom_call_target="tpu_custom_call" | custom-call | tf_op jit(solution)/shard_map/pallas_call | solution.py:525

commit v3 on v2

--- a/solution.py
+++ b/solution.py
@@ -49,8 +49,8 @@
     bal_h, cor_h,
     pair_v, res_v, rbf_v, lhs_v, rin_v, sdof_v, sdin_v, mdof_v, proj_v, gt_v, rg_v, zg_v, st_v,
     zsf_v, zsin_v, neu_v, z_v, y_v, cinv_v, idrow_v, idcol_v, ecol_v, erow_v, t1_v, a_v,
-    c_v, cin_v, col_v, pxo_v, pxi_v, m_v, wcat_v, wacc_v, w32_v, w16_v, v32_v, v16_v,
-    base_v, part_v, tr_v, mm_v, ret_v, t_v, ab32_v, ab_v, cd_v, sw_v, sum_v, rpin_v, bal_v, gath_v, acc_v,
+    c_v, cin_v, col_v, pxo_v, pxi_v, m_v, w_v, zt_v, accy_v, w32_v, w16_v, v32_v, v16_v,
+    base_v, part_v, tr_v, mm_v, ret_v, t_v, ab32_v, ab_v, cd_v, sw_v, sum_v, rpin_v, x_v, acc_v, cor_v,
     loc_sem, sd_send, sd_recv, zs_send, zs_recv, c_send, c_recv, p1_send, p1_recv, fw_send, fw_recv,
     sw_send, sw_recv, cd_send, cd_recv, ab_send, ab_recv,
     ix_send, ix_recv, iz_send, iz_recv, px_send, px_recv, pz_send, pz_recv,
@@ -76,19 +76,31 @@
 
     mate = (s + 1 - 2 * core, g)
 
+    def local(src, dst, k):
+        return pltpu.make_async_copy(src, dst, loc_sem.at[k])
+
+    c_res = local(res_h.at[0], res_v, 0)
+    c_sd = local(sdof_h.at[0, 0], sdof_v, 1)
+    c_res.start()
+    c_sd.start()
+
     barrier = pltpu.get_barrier_semaphore()
-    greeted = [sub_dev(k) for k in REACH] + [row_dev(r) for r in range(1, ROW)]
+    greeted = [row_dev(r) for r in range(1, ROW)]
     greeted += [sub_dev(ROW * k) for k in range(1, PLANES)] + [grp_dev(k) for k in range(1, GROUPS)]
+    expected = len(greeted)
+    for k in REACH:
+        outside = (row + k < 0) if k < 0 else (row + k >= ROW)
+        expected = expected + jnp.where(outside, 1, 0)
+
+        @pl.when(outside)
+        def _():
+            pl.semaphore_signal(barrier, inc=1, device_id=sub_dev(k), device_id_type=MESH)
+
     for dev in greeted:
         pl.semaphore_signal(barrier, inc=1, device_id=dev, device_id_type=MESH)
 
-    def local(src, dst, k):
-        return pltpu.make_async_copy(src, dst, loc_sem.at[k])
-
     order = [lax.rem(g + r, GROUPS) for r in (0, 3, 1, 2)]
     cols = [pl.ds(pl.multiple_of(q * ROWS, 128), ROWS) for q in order]
-    c_res = local(res_h.at[0], res_v, 0)
-    c_sd = local(sdof_h.at[0, 0], sdof_v, 1)
     c_md = local(mdof_h.at[0, 0], mdof_v, 2)
     c_pair = local(pair_h.at[g], pair_v, 3)
     c_proj = [local(proj_h.at[0, 0, j], proj_v.at[j], 4 + j) for j in range(PAIRS)]
@@ -96,16 +108,11 @@
     c_ci = local(cinv_h, cinv_v, 9)
     c_y = [local(yb_h.at[0, :, cols[r]], y_v.at[r], 10 + r) for r in range(GROUPS)]
     c_n = [local(neu_h.at[0, :, cols[r]], neu_v.at[r], 14 + r) for r in range(GROUPS)]
-    for c in [c_res, c_sd, c_md, c_pair, c_z] + c_proj + [c_ci] + c_y + c_n:
-        c.start()
-
-    idrow_v[0] = jnp.full((8, 128), ids_s[0] * NC, I32)
-    idcol_v[0] = idrow_v[0]
     c_res.wait()
     rbf_v[...] = res_v[...].astype(BF16)
     c_sd.wait()
 
-    pl.semaphore_wait(barrier, len(greeted))
+    pl.semaphore_wait(barrier, expected)
 
     def rcopy(src, dst, ss, rs, dev):
         return pltpu.make_async_remote_copy(
@@ -129,6 +136,10 @@
     p1.append(rcopy(rbf_v, rin_v.at[3], p1_send.at[3], p1_recv.at[3], mate))
     for c in sd + p1:
         c.start()
+    for c in [c_z, c_md, c_pair] + c_proj + [c_ci] + c_y + c_n:
+        c.start()
+    idrow_v[0] = jnp.full((8, 128), ids_s[0] * NC, I32)
+    idcol_v[0] = idrow_v[0]
 
     ix = [rcopy(idrow_v.at[0], idrow_v.at[r], ix_send.at[r], ix_recv.at[r], row_dev(r)) for r in range(1, ROW)]
     iz = [
@@ -246,23 +257,6 @@
         mm_v[j, COLS:, :] = mlo
         ret_v[j] = mm_nt(mhi, proj_v[j]).astype(BF16)
 
-    for c in zs:
-        c.wait_recv()
-    cc = [rcopy(c_v.at[o], cin_v.at[o], c_send.at[o], c_recv.at[o], sub_dev(REACH[o])) for o in range(4)]
-    shares = []
-    for j in range(PAIRS):
-        zsel = jnp.zeros((NC, FS), BF16)
-        for o in range(4):
-            for k in range(2):
-                zsel = zsel + zsin_v[o, k] * jnp.tile(v16_v[j, o, k], (3, 6))
-        shares.append(mm_nt(zsel, ret_v[j]))
-    for o in range(4):
-        total = shares[0] * jnp.tile(v32_v[0, o], (6, 1))
-        for j in range(1, PAIRS):
-            total = total + shares[j] * jnp.tile(v32_v[j, o], (6, 1))
-        c_v[o] = (-0.5 * total).astype(BF16)
-        cc[o].start()
-
     swc, cdc, abc = [], [], []
     for ch in range(CHUNKS):
         swc.append(rcopy(ab_v.at[ch, 1 - core], sw_v.at[ch], sw_send.at[ch], sw_recv.at[ch], mate))
@@ -283,6 +277,31 @@
             mine = ab32_v[ch, q, pl.ds(pl.multiple_of(core * HALF, HALF), HALF), :]
             sum_v[ch, q] = (mine + sw_v[ch, q].astype(F32)).astype(BF16)
             abc[ch][q].start()
+
+    cc = [rcopy(c_v.at[o], cin_v.at[o], c_send.at[o], c_recv.at[o], sub_dev(REACH[o])) for o in range(4)]
+
+    def own_share():
+        part = jnp.zeros((2 * NC, 2 * COLS), F32)
+        for j in range(PAIRS):
+            part = part + mm_nt(zg_v[j], mm_v[j])
+        part_v[...] += 0.5 * (part[:NC, :COLS] + part[NC:, :COLS] + part[:NC, COLS:])
+
+    def share():
+        for c in zs:
+            c.wait_recv()
+        shares = []
+        for j in range(PAIRS):
+            zsel = jnp.zeros((NC, FS), BF16)
+            for o in range(4):
+                for k in range(2):
+                    zsel = zsel + zsin_v[o, k] * jnp.tile(v16_v[j, o, k], (3, 6))
+            shares.append(mm_nt(zsel, ret_v[j]))
+        for o in range(4):
+            total = shares[0] * jnp.tile(v32_v[0, o], (6, 1))
+            for j in range(1, PAIRS):
+                total = total + shares[j] * jnp.tile(v32_v[j, o], (6, 1))
+            c_v[o] = (-0.5 * total).astype(BF16)
+            cc[o].start()
 
     for ch in range(CHUNKS):
         for j in range(PAIRS):
@@ -301,7 +320,10 @@
                 swc[ch].start()
         cdc[ch][0].start()
         cdc[ch][1].start()
-        if ch > 0:
+        if ch == 0:
+            share()
+            own_share()
+        else:
             add_swapped(ch - 1)
     add_swapped(CHUNKS - 1)
 
@@ -312,12 +334,7 @@
             moved = moved + mm_nt(mm_v[j], gt_v[j, at, :])
         base_v[:, at] = res_v[:, at] + 0.5 * (moved[:COLS] + moved[COLS:])
 
-    scatter(0)
-
-    part = jnp.zeros((2 * NC, 2 * COLS), F32)
-    for j in range(PAIRS):
-        part = part + mm_nt(zg_v[j], mm_v[j])
-    part = part_v[...] + 0.5 * (part[:NC, :COLS] + part[NC:, :COLS] + part[:NC, COLS:])
+    part = part_v[...]
     for o in range(4):
         cc[o].wait_recv()
         part = part + cin_v[o].astype(F32)
@@ -330,17 +347,18 @@
         c.start()
 
     def gcopy(src, ch, slot, h, k, step):
-        return rcopy(half(src, h), half(gath_v.at[slot, ch], h), g_send.at[ch, k], g_recv.at[ch, k], grp_dev(step))
+        part_of = (pl.ds(h * HALF, HALF), pl.ds(ch * CW, CW))
+        return rcopy(x_v.at[(src,) + part_of], x_v.at[(slot,) + part_of], g_send.at[ch, k], g_recv.at[ch, k], grp_dev(step))
 
     gat = []
     for ch in range(CHUNKS):
         gat.append([
-            gcopy(bal_v.at[ch], ch, 0, 0, 0, 1),
-            gcopy(bal_v.at[ch], ch, 1, 1, 1, 3),
-            gcopy(bal_v.at[ch], ch, 0, 1, 2, 1),
-            gcopy(bal_v.at[ch], ch, 1, 0, 3, 3),
-            gcopy(gath_v.at[0, ch], ch, 2, 0, 4, 1),
-            gcopy(gath_v.at[1, ch], ch, 2, 1, 5, 3),
+            gcopy(0, ch, 1, 0, 0, 1),
+            gcopy(0, ch, 2, 1, 1, 3),
+            gcopy(0, ch, 1, 1, 2, 1),
+            gcopy(0, ch, 2, 0, 3, 3),
+            gcopy(1, ch, 3, 0, 4, 1),
+            gcopy(2, ch, 3, 1, 5, 3),
         ])
 
     def balance(ch):
@@ -352,7 +370,7 @@
         back = rpin_v[0, ch].astype(F32) + rpin_v[1, ch].astype(F32) + rpin_v[2, ch].astype(F32)
         new = base_v[:, at] - 0.5 * back
         base_v[:, at] = new
-        bal_v[ch] = new.astype(BF16)
+        x_v[0, pl.ds(0, COLS), at] = new.astype(BF16)
         for k in range(4):
             gat[ch][k].start()
 
@@ -362,13 +380,13 @@
         gat[ch][1].wait_recv()
         gat[ch][5].start()
 
-    def solve(block, ch, x):
-        return mm_nt(x, neu_v[block, :, pl.ds(ch * CW, CW)])
-
+    def solve(block):
+        return mm_nt(neu_v[block], x_v[block])
+
+    scatter(0)
     balance(0)
     scatter(1)
     balance(1)
-    scatter(2)
 
     for c in pz:
         c.wait()
@@ -379,25 +397,18 @@
     px = [rcopy(pxo_v.at[r], pxi_v.at[r], px_send.at[r], px_recv.at[r], row_dev(r)) for r in range(1, ROW)]
     for c in px:
         c.start()
+    scatter(2)
     balance(2)
     c_bal = local(base_v, bal_h.at[0], 18)
     c_bal.start()
-
+    forward(0)
+    for c in c_y + c_n:
+        c.wait()
     for r in range(GROUPS):
-        c_y[r].wait()
-        c_n[r].wait()
-        yhi, ylo = split(y_v[r])
-        t = mm_nt(jnp.concatenate([yhi, ylo], 0), neu_v[r])
-        if r == 0:
-            wacc_v[...] = t
-        else:
-            wacc_v[...] += t
-    whi, wlo = split(z_v[...] - wacc_v[0:NC, :] - wacc_v[NC:, :])
-    wcat_v[0:NC, :] = whi
-    wcat_v[NC : 2 * NC, :] = whi
-    wcat_v[2 * NC :, :] = wlo
-
-    forward(0)
+        x_v[r, pl.ds(COLS, NC), :] = y_v[r].astype(BF16)
+    zt_v[...] = z_v[...].T
+
+    accy_v[...] = mm_nt(neu_v[3], x_v[3, pl.ds(COLS, NC), :])
     forward(1)
     mine = pxo_v[0].astype(F32)
     for r in range(1, ROW):
@@ -407,23 +418,29 @@
     mc = [rcopy(m_v.at[0], m_v.at[r], m_send.at[r], m_recv.at[r], grp_dev(r)) for r in range(1, 4)]
     for c in mc:
         c.start()
-    acc_v[...] = solve(0, 0, bal_v[0])
-    acc_v[...] += solve(0, 1, bal_v[1])
+    acc_v[...] = solve(0)
     forward(2)
-    acc_v[...] += solve(0, 2, bal_v[2])
-    for ch in range(CHUNKS):
-        for q in range(2):
+    for q in range(2):
+        for ch in range(CHUNKS):
             gat[ch][2 + q].wait_recv()
-            acc_v[...] += solve(1 + q, ch, gath_v[q, ch])
+        acc_v[...] += solve(1 + q)
+    w_v[...] = (zt_v[...] - accy_v[...] - acc_v[:, pl.ds(COLS, NC)]).astype(BF16)
+    for ch in range(CHUNKS - 1):
+        gat[ch][4].wait_recv()
+        gat[ch][5].wait_recv()
+    early = pl.ds(0, (CHUNKS - 1) * CW)
+    total = acc_v[:, 0:COLS] + mm_nt(neu_v[3, :, early], x_v[3, pl.ds(0, COLS), early])
     for c in mc:
         c.wait()
-    mhi, mlo = split((m_v[0] + m_v[1] + m_v[2] + m_v[3]).T)
-    acc_v[...] += mm_nn(jnp.concatenate([mhi, mlo, mhi], 1), wcat_v[...])
-    for ch in range(CHUNKS):
-        gat[ch][4].wait_recv()
-        gat[ch][5].wait_recv()
-        acc_v[...] += solve(3, ch, gath_v[2, ch])
-    c_cor = local(acc_v, cor_h.at[0], 19)
+    mhi, mlo = split(m_v[0] + m_v[1] + m_v[2] + m_v[3])
+    from_m = mm_nn(w_v[...], jnp.concatenate([mhi, mlo], 1))
+    acc_v[:, 0:COLS] = total + from_m[:, :COLS] + from_m[:, COLS:]
+    gat[CHUNKS - 1][4].wait_recv()
+    gat[CHUNKS - 1][5].wait_recv()
+    late = pl.ds((CHUNKS - 1) * CW, CW)
+    total = acc_v[:, 0:COLS] + mm_nt(neu_v[3, :, late], x_v[3, pl.ds(0, COLS), late])
+    cor_v[...] = total.T
+    c_cor = local(cor_v, cor_h.at[0], 19)
     c_cor.start()
     for c in sd + zs + cc + p1 + fw + swc:
         c.wait_send()
@@ -479,8 +496,9 @@
         vm((ROW, NC, COLS), BF16),
         vm((ROW, NC, COLS), BF16),
         vm((GROUPS, NC, COLS), F32),
-        vm((3 * NC, ROWS), BF16),
-        vm((2 * NC, ROWS), F32),
+        vm((ROWS, NC), BF16),
+        vm((ROWS, NC), F32),
+        vm((ROWS, NC), F32),
         vm((PAIRS, 4, 8, 128), F32),
         vm((PAIRS, 4, 16, 128), BF16),
         vm((PAIRS, 4, 8, 128), F32),
@@ -497,8 +515,8 @@
         vm((CHUNKS, 2, HALF, CW), BF16),
         vm((CHUNKS, 2, HALF, CW), BF16),
         vm((3, CHUNKS, COLS, CW), BF16),
-        vm((CHUNKS, COLS, CW), BF16),
-        vm((3, CHUNKS, COLS, CW), BF16),
+        vm((GROUPS, COLS + NC, ROWS), BF16),
+        vm((ROWS, COLS + NC), F32),
         vm((COLS, ROWS), F32),
         dma((20,)),
         dma((4,)), dma((4,)), dma((4,)), dma((4,)), dma((4,)), dma((4,)),

time: 57.4 us -> 54.7 us (0.953)
  Pallas kernels: 56 us -> 53.2 us
    pallas_call x1, Pallas kernels: 53.7 us -> 51 us  [local_part(): pl.pallas_call(kernel, out_shape=(region, region), in_specs=[any_spec, sm...]
where the time goes in v3:
time: 54.7 us; the launch traced here: 54.5 us
  Pallas kernels  53.2 us (97%)
  between operations  1.29 us (2%)
    pallas_call x1, Pallas kernels, local_part(): pl.pallas_call(kernel, out_shape=(region, region), in_specs=[any_spec, sm...  51 us
    pallas_call x1, Pallas kernels, local_part(): pl.pallas_call(hand_over, out_shape=(region, region), in_specs=[whole, wh...  2.29 us

profile of v3, /device:TPU:0, one launch (start us, length us, event | category | flops | bytes accessed | tf_op | source)
XLA Modules:
  0.0 54.5 jit_solution(13205321885434774072)
XLA Ops:
  1.3 51.0 %shard_map.113 = (f32[1,128,1152]{2,1,0:T(8,128)}, f32[1,128,1152]{2,1,0:T(8,128)}) custom-call(s32[4,4,2,32]{3,2,1,0:T(2,128)} %bitcast.1, s32[1]{0:T(128)S(6)} %copy.12.ids_s, f32[1,128,1152]{2,1,0:T(8,128)} %res_h.1, bf16[1,1152,4608]{2,1,0:T(8,128)(2,1)} %neu_h.1, bf16[1,1,4,768,1024]{4,3,2,1,0:T(8,128)(2,1)} %proj_h.1, s32[1,1,2,768]{3,2,1,0:T(2,128)} %sdof_h.1, ...), custom_call_target="tpu_custom_call" | custom-call | tf_op jit(solution)/shard_map/pallas_call | solution.py:529
  52.2 2.3 %shard_map.114 = (f32[1,128,1152]{2,1,0:T(8,128)}, f32[1,128,1152]{2,1,0:T(8,128)}) custom-call(f32[1,128,1152]{2,1,0:T(8,128)} %get-tuple-element.4.a_ref, f32[1,128,1152]{2,1,0:T(8,128)} %get-tuple-element.5.b_ref), custom_call_target="tpu_custom_call" | custom-call | tf_op jit(solution)/shard_map/pallas_call | solution.py:543

commit v4 on v3

--- a/solution.py
+++ b/solution.py
@@ -322,10 +322,10 @@
         cdc[ch][1].start()
         if ch == 0:
             share()
+            add_swapped(0)
             own_share()
-        else:
-            add_swapped(ch - 1)
-    add_swapped(CHUNKS - 1)
+        elif ch == 2:
+            add_swapped(1)
 
     def scatter(ch):
         at = pl.ds(ch * CW, CW)
@@ -334,17 +334,8 @@
             moved = moved + mm_nt(mm_v[j], gt_v[j, at, :])
         base_v[:, at] = res_v[:, at] + 0.5 * (moved[:COLS] + moved[COLS:])
 
-    part = part_v[...]
-    for o in range(4):
-        cc[o].wait_recv()
-        part = part + cin_v[o].astype(F32)
-    col_v[0] = part.astype(BF16)
-    pz = [
-        rcopy(col_v.at[0], col_v.at[k], pz_send.at[k], pz_recv.at[k], sub_dev(ROW * k))
-        for k in range(1, PLANES)
-    ]
-    for c in pz:
-        c.start()
+    scatter(0)
+    add_swapped(CHUNKS - 1)
 
     def gcopy(src, ch, slot, h, k, step):
         part_of = (pl.ds(h * HALF, HALF), pl.ds(ch * CW, CW))
@@ -383,8 +374,19 @@
     def solve(block):
         return mm_nt(neu_v[block], x_v[block])
 
-    scatter(0)
     balance(0)
+
+    part = part_v[...]
+    for o in range(4):
+        cc[o].wait_recv()
+        part = part + cin_v[o].astype(F32)
+    col_v[0] = part.astype(BF16)
+    pz = [
+        rcopy(col_v.at[0], col_v.at[k], pz_send.at[k], pz_recv.at[k], sub_dev(ROW * k))
+        for k in range(1, PLANES)
+    ]
+    for c in pz:
+        c.start()
     scatter(1)
     balance(1)
 

time: 54.7 us -> 54.2 us (level)
  no operation moved by 1% of the time
where the time goes in v4:
time: 54.2 us; the launch traced here: 54 us
  Pallas kernels  52.7 us (97%)
  between operations  1.29 us (2%)
    pallas_call x1, Pallas kernels, local_part(): pl.pallas_call(kernel, out_shape=(region, region), in_specs=[any_spec, sm...  50.4 us
    pallas_call x1, Pallas kernels, local_part(): pl.pallas_call(hand_over, out_shape=(region, region), in_specs=[whole, wh...  2.29 us

profile of v4, /device:TPU:0, one launch (start us, length us, event | category | flops | bytes accessed | tf_op | source)
XLA Modules:
  0.0 54.0 jit_solution(1032300777989574940)
XLA Ops:
  1.3 50.4 %shard_map.113 = (f32[1,128,1152]{2,1,0:T(8,128)}, f32[1,128,1152]{2,1,0:T(8,128)}) custom-call(s32[4,4,2,32]{3,2,1,0:T(2,128)} %bitcast.1, s32[1]{0:T(128)S(6)} %copy.12.ids_s, f32[1,128,1152]{2,1,0:T(8,128)} %res_h.1, bf16[1,1152,4608]{2,1,0:T(8,128)(2,1)} %neu_h.1, bf16[1,1,4,768,1024]{4,3,2,1,0:T(8,128)(2,1)} %proj_h.1, s32[1,1,2,768]{3,2,1,0:T(2,128)} %sdof_h.1, ...), custom_call_target="tpu_custom_call" | custom-call | tf_op jit(solution)/shard_map/pallas_call | solution.py:531
  51.7 2.3 %shard_map.114 = (f32[1,128,1152]{2,1,0:T(8,128)}, f32[1,128,1152]{2,1,0:T(8,128)}) custom-call(f32[1,128,1152]{2,1,0:T(8,128)} %get-tuple-element.4.a_ref, f32[1,128,1152]{2,1,0:T(8,128)} %get-tuple-element.5.b_ref), custom_call_target="tpu_custom_call" | custom-call | tf_op jit(solution)/shard_map/pallas_call | solution.py:545
